TPU v7x, 256 devices: a whole 4x4x8 slice. The times are simulated.
256 devices in a mesh: row: 8 (over y, core), tm: 32 (over x, z).
Axes of the slice: x: 4, y: 4, z: 8, core: 2. Of those that a mesh axis runs over, the one named last changes fastest.
Arguments:
- residual: float32 [128, 1024, 1024], P('tm', 'row'), may hold values from -40 to 40, as said below
- direction: float32 [128, 1024, 1024], P('tm', 'row'), may hold values from -40 to 40, as said below
- observed: int32 [128, 1024, 1024], P('tm', 'row'), may hold values 0 or 1
- obs_weight: float32 [1024, 1024], P('row'), may hold values from 0.5 to 8
- ocean_blocks: int32 [128, 128], replicated, may hold values 0 or 1
- previous_dot: float32 [1], replicated, may hold values from 1 to 8
Outputs:
- residual_new: float32 [128, 1024, 1024], P('tm', 'row')
- precond: float32 [128, 1024, 1024], P('tm', 'row')
Inputs may be any that keep to these rules, and one draw needn't show every extreme that they name: `residual`: a rough field whose magnitude varies by rows and hours over about two decades. `direction`: a rough field whose magnitude varies by rows and hours over about two decades.
All inputs are finite; a program needn't handle non-finite values. No bound on the sum of `observed` on one device may be relied on, other than what follows from the above.
Results may differ from a plain program's by a relative error of at most 0.0003.
Values sent between devices are 32-bit elements; how exact they have to be, the bound alone decides.
A program may use at most 192 MiB of HBM per device.

v0:
```python
import functools
import math

import jax
import jax.numpy as jnp
import ml_dtypes
import numpy as np
from jax import lax
from jax.experimental import pallas as pl
from jax.experimental.pallas import tpu as pltpu
from jax.sharding import PartitionSpec as P

MESH = pl.DeviceIdType.MESH
BF16 = jnp.bfloat16
F32 = jnp.float32

BLOCK = 8
NUGGET = 0.25
COUPLING = 50.0
PRECOND_SHIFT = 0.5

N = 1024
NT = 128
ROWS = 8
TM = 32
HOURS = NT // TM
BAND = N // ROWS
CHUNKS = 4
CK = BAND // CHUNKS
M = HOURS * CK
FRONT = HOURS * BAND

NN = (((1,), (0,)), ((), ()))
NT_DIMS = (((1,), (1,)), ((), ()))


def split_np(table):
    high = table.astype(ml_dtypes.bfloat16)
    low = (table - high.astype(np.float64)).astype(ml_dtypes.bfloat16)
    return np.stack([high, low])


def tables():
    def cas(freq, count):
        phase = (freq[:, None] * np.arange(count)[None, :]) % N
        angle = phase * (2.0 * math.pi / N)
        return np.cos(angle) + np.sin(angle)

    four = 4 * np.arange(N // 4)
    two = four + 2
    odd = 2 * np.arange(N // 2) + 1
    even_table = np.stack([split_np(cas(four, N // 4)), split_np(cas(two, N // 4))])
    odd_table = split_np(cas(odd, N // 2))
    order = np.concatenate([four, two, odd])
    lam = (2.0 - 2.0 * np.cos(order * (2.0 * math.pi / N))).astype(np.float32)
    lam_rows = np.broadcast_to(lam.reshape(8, 1, 128), (8, 8, 128)).copy()
    lam_cols = np.broadcast_to(lam[:, None], (N, 128)).copy()
    return even_table, odd_table, lam_rows, lam_cols


def dot3(a_hi, a_lo, b_hi, b_lo, dims):
    def one(a, b):
        return lax.dot_general(a, b, dims, preferred_element_type=F32)

    return one(a_hi, b_hi) + (one(a_hi, b_lo) + one(a_lo, b_hi))


def split(value):
    high = value.astype(BF16)
    low = (value - high.astype(F32)).astype(BF16)
    return high, low


def decay(eigen):
    a = (PRECOND_SHIFT + eigen) * (1.0 / COUPLING)
    root = jnp.sqrt(a * a + 4.0 * a)
    return 2.0 / (a + 2.0 + root)


def freq_start(row, chunk):
    odd = row // 4
    even = 1 - odd
    half = (row // 2) % 2
    start = odd * (512 + chunk * (4 * CK) + (row - 4) * CK) + even * (
        half * 256 + chunk * (2 * CK) + (row % 2) * CK
    )
    return pl.multiple_of(start, CK)


def solve_kernel(
    res, te, to, lam_rows, lam_cols, y,
    r_even, r_odd, v_even, v_odd, send_a, recv_a, spec, fg, own, back, inc, send_w,
    sem_sa, sem_ra, sem_sf, sem_rf, sem_sb, sem_rb, sem_sw, sem_rw,
):
    row = lax.axis_index("row")
    tm = lax.axis_index("tm")

    barrier = pltpu.get_barrier_semaphore()

    @pl.loop(1, ROWS)
    def _(o):
        pl.semaphore_signal(
            barrier, inc=1, device_id={"row": lax.rem(row + o, ROWS)}, device_id_type=MESH
        )

    @pl.loop(1, TM)
    def _(o):
        pl.semaphore_signal(
            barrier, inc=1, device_id={"tm": lax.rem(tm + o, TM)}, device_id_type=MESH
        )

    for h in range(HOURS):
        rows = slice(h * BAND, (h + 1) * BAND)
        low = res[rows, 0:512]
        high = res[rows, 512:1024]
        hi, lo = split(low - high)
        r_odd[0, rows, :] = hi
        r_odd[1, rows, :] = lo
        even = low + high
        for s, value in ((0, even[:, :256] + even[:, 256:]), (1, even[:, :256] - even[:, 256:])):
            hi, lo = split(value)
            r_even[s, 0, rows, :] = hi
            r_even[s, 1, rows, :] = lo

    pl.semaphore_wait(barrier, ROWS - 1 + TM - 1)

    def stage_a(c):
        part = pl.ds(pl.multiple_of(c * (4 * CK), 4 * CK), 4 * CK)
        out = dot3(to[0, part, :], to[1, part, :], r_odd[0], r_odd[1], NT_DIMS)
        for r in range(4):
            send_a[c, 4 + r] = out[r * CK:(r + 1) * CK]
        part = pl.ds(pl.multiple_of(c * (2 * CK), 2 * CK), 2 * CK)
        for s in range(2):
            out = dot3(
                te[s, 0, part, :], te[s, 1, part, :], r_even[s, 0], r_even[s, 1], NT_DIMS
            )
            for r in range(2):
                send_a[c, 2 * s + r] = out[r * CK:(r + 1) * CK]
        recv_a[c, row] = send_a[c, row]

        @pl.loop(1, ROWS)
        def _(o):
            peer = lax.rem(row + o, ROWS)
            pltpu.make_async_remote_copy(
                src_ref=send_a.at[c, peer],
                dst_ref=recv_a.at[c, row],
                send_sem=sem_sa.at[c],
                recv_sem=sem_ra.at[c],
                device_id={"row": peer},
                device_id_type=MESH,
            ).start()

    def wait_for(ref, sem):
        pltpu.make_async_copy(ref, ref, sem).wait()

    def stage_b(c):
        wait_for(recv_a.at[c, pl.ds(0, ROWS - 1)], sem_ra.at[c])
        for h in range(HOURS):
            rows = slice(h * CK, (h + 1) * CK)
            lanes = slice(h * BAND, (h + 1) * BAND)
            v = [recv_a[c, r, :, lanes] for r in range(ROWS)]
            e = [v[r] + v[r + 4] for r in range(4)]
            for r in range(4):
                hi, lo = split(v[r] - v[r + 4])
                v_odd[0, rows, r * BAND:(r + 1) * BAND] = hi
                v_odd[1, rows, r * BAND:(r + 1) * BAND] = lo
            for r in range(2):
                for s, value in ((0, e[r] + e[r + 2]), (1, e[r] - e[r + 2])):
                    hi, lo = split(value)
                    v_even[s, 0, rows, r * BAND:(r + 1) * BAND] = hi
                    v_even[s, 1, rows, r * BAND:(r + 1) * BAND] = lo
        spec[c, :, 512:1024] = dot3(v_odd[0], v_odd[1], to[0], to[1], NT_DIMS)
        for s in range(2):
            spec[c, :, s * 256:(s + 1) * 256] = dot3(
                v_even[s, 0], v_even[s, 1], te[s, 0], te[s, 1], NT_DIMS
            )

    def chunk_decay(c, q):
        start = pl.multiple_of(freq_start(row, c) + q * 8, 8)
        col = lam_cols[pl.ds(start, 8), :]
        return jnp.concatenate([decay(lam_rows[l] + col) for l in range(8)], axis=1)

    def stage_c(c):
        for q in range(CK // 8):
            rho = chunk_decay(c, q)
            b = [spec[c, h * CK + q * 8:h * CK + q * 8 + 8, :] for h in range(HOURS)]
            f = b[3] + rho * (b[2] + rho * (b[1] + rho * b[0]))
            g = b[0] + rho * (b[1] + rho * (b[2] + rho * b[3]))
            for l in range(8):
                fg[c, q * 8 + l, 0:8, :] = f[:, l * 128:(l + 1) * 128]
                fg[c, q * 8 + l, 8:16, :] = g[:, l * 128:(l + 1) * 128]
        own[c, tm] = fg[c, tm]

        @pl.loop(1, TM)
        def _(o):
            peer = lax.rem(tm + o, TM)
            pltpu.make_async_remote_copy(
                src_ref=fg.at[c, peer],
                dst_ref=own.at[c, tm],
                send_sem=sem_sf.at[c],
                recv_sem=sem_rf.at[c],
                device_id={"tm": peer},
                device_id_type=MESH,
            ).start()

    def stage_d(c):
        wait_for(own.at[c, pl.ds(0, TM - 1)], sem_rf.at[c])
        start = pl.multiple_of(freq_start(row, c) + (tm // 8) * 8, 8)
        rho = decay(lam_rows[tm % 8] + lam_cols[pl.ds(start, 8), :])
        rho2 = rho * rho
        rho4 = rho2 * rho2
        whole = rho4
        for _ in range(5):
            whole = whole * whole
        zero = jnp.zeros((8, 128), F32)

        def sums(d, carry):
            p, q = carry
            return own[c, d, 0:8, :] + rho4 * p, own[c, TM - 1 - d, 8:16, :] + rho4 * q

        right, left = lax.fori_loop(0, TM, sums, (zero, zero), unroll=8)
        scale = 1.0 / (1.0 - whole * whole)
        p = (left + whole * right) * scale
        q = (right + whole * left) * scale

        def starts(d, carry):
            p, q = carry
            back[c, d, 0:8, :] = p
            back[c, TM - 1 - d, 8:16, :] = q
            return own[c, d, 0:8, :] + rho4 * p, own[c, TM - 1 - d, 8:16, :] + rho4 * q

        lax.fori_loop(0, TM, starts, (p, q), unroll=8)
        inc[c, tm] = back[c, tm]

        @pl.loop(1, TM)
        def _(o):
            peer = lax.rem(tm + o, TM)
            pltpu.make_async_remote_copy(
                src_ref=back.at[c, peer],
                dst_ref=inc.at[c, tm],
                send_sem=sem_sb.at[c],
                recv_sem=sem_rb.at[c],
                device_id={"tm": peer},
                device_id_type=MESH,
            ).start()

    def stage_e(c):
        wait_for(inc.at[c, pl.ds(0, TM - 1)], sem_rb.at[c])
        for q in range(CK // 8):
            rho = chunk_decay(c, q)
            f = jnp.concatenate([inc[c, q * 8 + l, 0:8, :] for l in range(8)], axis=1)
            g = jnp.concatenate([inc[c, q * 8 + l, 8:16, :] for l in range(8)], axis=1)
            scale = rho / (1.0 - rho * rho) * (1.0 / float(N * N))
            b = [spec[c, h * CK + q * 8:h * CK + q * 8 + 8, :] for h in range(HOURS)]
            later = [None] * HOURS
            g = rho * g
            for h in range(HOURS - 1, -1, -1):
                later[h] = g
                if h:
                    g = rho * (b[h] + g)
            for h in range(HOURS):
                f = b[h] + rho * f
                spec[c, h * CK + q * 8:h * CK + q * 8 + 8, :] = scale * (f + later[h])

    def stage_f(c):
        hi, lo = split(spec[c, :, 512:1024])
        odd = dot3(hi, lo, to[0], to[1], NN)
        parts = []
        for s in range(2):
            hi, lo = split(spec[c, :, s * 256:(s + 1) * 256])
            parts.append(dot3(hi, lo, te[s, 0], te[s, 1], NN))
        even = jnp.concatenate([parts[0] + parts[1], parts[0] - parts[1]], axis=1)
        for half, value in ((0, even + odd), (1, even - odd)):
            for r in range(4):
                for h in range(HOURS):
                    send_w[c, 4 * half + r, :, h * BAND:(h + 1) * BAND] = value[
                        h * CK:(h + 1) * CK, r * BAND:(r + 1) * BAND
                    ]
        here = pl.ds(freq_start(row, c), CK)
        y[here, :] = send_w[c, row]

        @pl.loop(1, ROWS)
        def _(o):
            peer = lax.rem(row + o, ROWS)
            pltpu.make_async_remote_copy(
                src_ref=send_w.at[c, peer],
                dst_ref=y.at[here, :],
                send_sem=sem_sw.at[c],
                recv_sem=sem_rw.at[c],
                device_id={"row": peer},
                device_id_type=MESH,
            ).start()

    @pl.loop(0, CHUNKS)
    def _(c):
        stage_a(c)

    @pl.loop(0, CHUNKS + 2)
    def _(i):
        @pl.when(i < CHUNKS)
        def _():
            stage_b(i)
            stage_c(i)

        @pl.when((i >= 1) & (i < CHUNKS + 1))
        def _():
            stage_d(i - 1)

        @pl.when(i >= 2)
        def _():
            stage_e(i - 2)
            stage_f(i - 2)

    @pl.loop(0, CHUNKS)
    def _(c):
        wait_for(send_a.at[c, pl.ds(0, ROWS - 1)], sem_sa.at[c])
        wait_for(fg.at[c, pl.ds(0, TM - 1)], sem_sf.at[c])
        wait_for(back.at[c, pl.ds(0, TM - 1)], sem_sb.at[c])
        wait_for(send_w.at[c, pl.ds(0, ROWS - 1)], sem_sw.at[c])
        wait_for(send_w.at[c, pl.ds(0, ROWS - 1)], sem_rw.at[c])


def spectral_solve(res, te, to, lam_rows, lam_cols):
    vmem = pl.BlockSpec(memory_space=pltpu.VMEM)
    return pl.pallas_call(
        solve_kernel,
        out_shape=jax.ShapeDtypeStruct((N, FRONT), F32),
        in_specs=[vmem] * 5,
        out_specs=vmem,
        scratch_shapes=[
            pltpu.VMEM((2, 2, FRONT, 256), BF16),
            pltpu.VMEM((2, FRONT, 512), BF16),
            pltpu.VMEM((2, 2, M, 256), BF16),
            pltpu.VMEM((2, M, 512), BF16),
            pltpu.VMEM((CHUNKS, ROWS, CK, FRONT), F32),
            pltpu.VMEM((CHUNKS, ROWS, CK, FRONT), F32),
            pltpu.VMEM((CHUNKS, M, N), F32),
            pltpu.VMEM((CHUNKS, TM, 16, 128), F32),
            pltpu.VMEM((CHUNKS, TM, 16, 128), F32),
            pltpu.VMEM((CHUNKS, TM, 16, 128), F32),
            pltpu.VMEM((CHUNKS, TM, 16, 128), F32),
            pltpu.VMEM((CHUNKS, ROWS, CK, FRONT), F32),
        ]
        + [pltpu.SemaphoreType.DMA((CHUNKS,))] * 8,
        compiler_params=pltpu.CompilerParams(
            collective_id=1, has_side_effects=True, vmem_limit_bytes=48 * 1024 * 1024
        ),
        name="spectral_solve",
    )(res, te, to, lam_rows, lam_cols)


def finish_kernel(y, te, to, out):
    value = y[...].T
    hi, lo = split(value[:, 512:1024])
    odd = dot3(hi, lo, to[0], to[1], NN)
    parts = []
    for s in range(2):
        hi, lo = split(value[:, s * 256:(s + 1) * 256])
        parts.append(dot3(hi, lo, te[s, 0], te[s, 1], NN))
    even = jnp.concatenate([parts[0] + parts[1], parts[0] - parts[1]], axis=1)
    out[0, :, 0:512] = even + odd
    out[0, :, 512:1024] = even - odd


def finish(y, te, to):
    return pl.pallas_call(
        finish_kernel,
        grid=(HOURS,),
        out_shape=jax.ShapeDtypeStruct((HOURS, BAND, N), F32),
        in_specs=[
            pl.BlockSpec((N, BAND), lambda h: (0, h)),
            pl.BlockSpec((2, 2, 256, 256), lambda h: (0, 0, 0, 0)),
            pl.BlockSpec((2, 512, 512), lambda h: (0, 0, 0)),
        ],
        out_specs=pl.BlockSpec((1, BAND, N), lambda h: (h, 0, 0)),
        compiler_params=pltpu.CompilerParams(vmem_limit_bytes=48 * 1024 * 1024),
        name="finish",
    )(y, te, to)


def extended_2(block, sides, width):
    for axis, dim in sides:
        count = lax.axis_size(axis)
        forward = [(i, i + 1) for i in range(count - 1)]
        backward = [(target, source) for source, target in forward]
        low = lax.ppermute(
            lax.slice_in_dim(block, block.shape[dim] - width, None, axis=dim), axis, forward
        )
        high = lax.ppermute(lax.slice_in_dim(block, 0, width, axis=dim), axis, backward)
        block = jnp.concatenate([low, block, high], axis=dim)
    return block


def per_device(residual, direction, observed, obs_weight, ocean_blocks, previous_dot):
    hours, rows, cols = direction.shape
    row_index = lax.axis_index("row")
    hour_index = lax.axis_index("tm")
    row_count = lax.axis_size("row")
    hour_count = lax.axis_size("tm")
    total_hours = hours * hour_count
    total_rows = rows * row_count
    widened = jnp.repeat(ocean_blocks, BLOCK, axis=1).astype(jnp.float32)
    padded_blocks = jnp.pad(widened, ((1, 1), (0, 0)))
    cell_rows = jnp.repeat(padded_blocks, BLOCK, axis=0)
    ocean_rim = lax.dynamic_slice_in_dim(cell_rows, row_index * rows + BLOCK - 1, rows + 2, 0)
    ocean = ocean_rim[1:-1]
    north_link = ocean * ocean_rim[:-2]
    south_link = ocean * ocean_rim[2:]
    east_link = ocean * jnp.roll(ocean, -1, axis=1)
    west_link = ocean * jnp.roll(ocean, 1, axis=1)
    extended = extended_2(direction, (("row", 1), ("tm", 0)), 1)
    time_prev = extended[:-2, 1:-1]
    time_next = extended[2:, 1:-1]
    north = extended[1:-1, :-2]
    south = extended[1:-1, 2:]
    east = jnp.roll(direction, -1, axis=2)
    west = jnp.roll(direction, 1, axis=2)
    hour_ids = hour_index * hours + jnp.arange(hours, dtype=jnp.int32)
    has_prev = (hour_ids > 0).astype(jnp.float32)[:, None, None]
    has_next = (hour_ids < total_hours - 1).astype(jnp.float32)[:, None, None]
    temporal = has_prev * (direction - time_prev) + has_next * (direction - time_next)
    weight = observed.astype(jnp.float32) * ocean * obs_weight + NUGGET
    spatial = (
        north_link * (direction - north)
        + south_link * (direction - south)
        + east_link * (direction - east)
        + west_link * (direction - west)
    )
    image = weight * direction + spatial + COUPLING * temporal
    total_dot = lax.psum(jnp.sum(direction * image), ("row", "tm"))
    alpha = previous_dot[0] / (total_dot / float(total_hours * total_rows * cols))
    residual_new = residual - alpha * image
    te, to, lam_rows, lam_cols = (jnp.asarray(t) for t in tables())
    y = spectral_solve(residual_new.reshape(FRONT, N), te, to, lam_rows, lam_cols)
    precond = finish(y, te, to)
    return (residual_new, precond)


def solution(mesh):
    in_specs = (
        P("tm", "row", None),
        P("tm", "row", None),
        P("tm", "row", None),
        P("row", None),
        P(),
        P(),
    )
    out_specs = (P("tm", "row", None), P("tm", "row", None))
    return jax.shard_map(
        per_device, mesh=mesh, in_specs=in_specs, out_specs=out_specs, check_vma=False
    )
```

profile of v0, /device:TPU:1, one launch (start us, length us, event | category | flops | bytes accessed | tf_op | source)
XLA Modules:
  0.0 205.8 jit_solution(12441932078374412293)
XLA Ops:
  0.6 1.0 fusion.21
  1.6 4.6 %collective-permute-start = (f32[4,1,1024]{2,1,0:T(1,128)S(1)}, f32[4,1,1024]{2,1,0:T(1,128)S(1)}, u32[]{:S(2)}, u32[]{:S(2)}) collective-permute-start(f32[4,1,1024]{2,1,0:T(1,128)S(1)} %get-tuple-element.16), channel_id=1, source_target_pairs={{0,32},{32,64},{64,96},{96,128},{128,160},{160,192},{192,224},{1,3... | collective-permute-start | bytes 49160 | tf_op jit(solution)/shard_map/ppermute | solution.py:386
  6.2 1.9 collective-permute-start.1
  8.2 0.8 convert_element_type.27
  9.0 0.1 copy.12
  9.2 0.2 copy.14
  9.4 0.6 broadcast_bitcast_fusion
  10.0 0.0 copy-start.5
  10.0 0.1 dynamic-slice_multiply_fusion.1
  10.1 1.9 copy-done.5
  12.0 1.1 fusion.18
  13.1 1.1 constant_dynamic-slice_fusion
  14.2 2.8 %dynamic-slice_multiply_fusion = (f32[128,1024]{1,0:T(8,128)}, f32[128,1024]{1,0:T(8,128)}, f32[128,1024]{1,0:T(8,128)}) fusion(f32[128,1024]{1,0:T(8,128)S(1)} %get-tuple-element.5, f32[1040,1024]{1,0:T(8,128)} %copy-done.5, s32[]{:T(128)S(6)} %add.62, f32[128,1]{1,0:T(8,128)S(1)} %get-tuple-element.8, f32[128,1023]{1,0:T(8,128)} %get-tuple-element.6, ...), kind=kLoop, calls=%fused_computation.33 | loop fusion | flops 655360 | bytes 3670020 | tf_op jit(solution)/shard_map/mul | solution.py:408
  17.0 0.0 collective-permute-done
  17.0 0.0 collective-permute-done.1
  17.0 0.0 copy-done.4
  17.0 1.1 pad_maximum_fusion.10
  18.1 4.4 %collective-permute-start.2 = (f32[1,130,1024]{2,1,0:T(8,128)}, f32[1,130,1024]{2,1,0:T(8,128)}, u32[]{:S(2)}, u32[]{:S(2)}) collective-permute-start(f32[1,130,1024]{2,1,0:T(8,128)} %get-tuple-element.10), channel_id=1, source_target_pairs={{0,1},{1,2},{2,3},{3,4},{4,5},{5,6},{6,7},{7,8},{8,9},{9,10},{10,1... | collective-permute-start | bytes 1597448 | tf_op jit(solution)/shard_map/ppermute | solution.py:386
  22.5 1.3 collective-permute-start.3
  23.8 0.8 fusion.20
  25.3 0.0 copy-start.6
  25.3 0.0 copy-start.7
  25.3 0.0 copy-start.8
  25.3 0.0 copy-start.9
  25.3 0.0 copy-start.10
  25.3 0.0 copy-start.11
  25.3 0.7 fusion.19
  26.1 6.8 %collective-permute-done.2 = f32[1,130,1024]{2,1,0:T(8,128)} collective-permute-done((f32[1,130,1024]{2,1,0:T(8,128)}, f32[1,130,1024]{2,1,0:T(8,128)}, u32[]{:S(2)}, u32[]{:S(2)}) %collective-permute-start.2) | collective-permute-done | bytes 532512 | tf_op jit(solution)/shard_map/ppermute | solution.py:386
  32.9 4.9 %collective-permute-done.3 = f32[1,130,1024]{2,1,0:T(8,128)} collective-permute-done((f32[1,130,1024]{2,1,0:T(8,128)}, f32[1,130,1024]{2,1,0:T(8,128)}, u32[]{:S(2)}, u32[]{:S(2)}) %collective-permute-start.3) | collective-permute-done | bytes 532512 | tf_op jit(solution)/shard_map/ppermute | solution.py:389
  37.8 0.0 copy-done.6
  37.8 0.0 copy-done.7
  37.8 0.0 copy-done.8
  37.8 0.0 copy-done.9
  37.8 0.0 copy-done.10
  37.8 0.0 copy-done.11
  37.8 6.0 %multiply_reduce_fusion = (f32[]{:T(128)}, f32[4,128,1024]{2,1,0:T(8,128)}) fusion(f32[4,128,1024]{2,1,0:T(8,128)S(1)} %copy-done.4, f32[1,130,1024]{2,1,0:T(8,128)} %collective-permute-done.3, f32[4,1,1024]{2,1,0:T(1,128)S(1)} %collective-permute-done.1, f32[4,1,1024]{2,1,0:T(1,128)S(1)} %collective-permute-done, f32[4]{0:T(128)S(1)} %get-tuple-element.21, ...), kind=kLoop, calls=%fused_computation.29 | loop fusion | flops 18874368 | bytes 14729252 | tf_op jit(solution)/shard_map/reduce_sum | solution.py:430
  43.8 79.3 %psum.7 = f32[]{:T(128)} all-reduce(f32[]{:T(128)} %get-tuple-element.2), channel_id=1, replica_groups=mesh['row'=8,'tm'=32] {'row','tm'}, use_global_device_ids=true, to_apply=%region_1.2 | all-reduce | flops 1 | bytes 8 | tf_op jit(solution)/shard_map/psum | solution.py:430
  123.9 0.0 copy-start
  123.9 0.0 copy-start.1
  123.9 0.0 copy-start.2
  123.9 0.0 copy-start.3
  123.9 4.3 %multiply_subtract_fusion = f32[4,128,1024]{2,1,0:T(8,128)} fusion(f32[4,128,1024]{2,1,0:T(8,128)} %param.10, f32[4,128,1024]{2,1,0:T(8,128)} %get-tuple-element.3, f32[]{:T(128)S(6)} %div.7), kind=kLoop, calls=%fused_computation.28 | loop fusion | flops 1048576 | bytes 6291460 | tf_op jit(solution)/shard_map/sub | solution.py:432
  128.2 0.0 copy-done
  128.2 0.0 copy-done.1
  128.2 0.0 copy-done.2
  128.2 0.0 copy-done.3
  128.3 74.1 %spectral_solve.1.y = f32[1024,512]{1,0:T(8,128)S(1)} custom-call(f32[512,1024]{1,0:T(8,128)} %bitcast.7, bf16[2,2,256,256]{3,2,1,0:T(8,128)(2,1)S(1)} %copy-done.1, bf16[2,512,512]{2,1,0:T(8,128)(2,1)S(1)} %copy-done, f32[8,8,128]{2,1,0:T(8,128)S(1)} %copy-done.3, f32[1024,128]{1,0:T(8,128)S(1)} %copy-done.2), custom_call_target="tpu_custom_call" | custom-call | tf_op jit(solution)/shard_map/spectral_solve/pallas_call | solution.py:325
  202.4 3.4 %finish.1 = f32[4,128,1024]{2,1,0:T(8,128)} custom-call(f32[1024,512]{1,0:T(8,128)S(1)} %spectral_solve.1.y, bf16[2,2,256,256]{3,2,1,0:T(8,128)(2,1)S(1)} %copy-done.1, bf16[2,512,512]{2,1,0:T(8,128)(2,1)S(1)} %copy-done), custom_call_target="tpu_custom_call" | custom-call | tf_op jit(solution)/shard_map/finish/pallas_call | solution.py:366
  (4 shorter events, 0.1 us)
Async XLA Ops:
  1.6 15.4 %collective-permute-start = (f32[4,1,1024]{2,1,0:T(1,128)S(1)}, f32[4,1,1024]{2,1,0:T(1,128)S(1)}, u32[]{:S(2)}, u32[]{:S(2)}) collective-permute-start(f32[4,1,1024]{2,1,0:T(1,128)S(1)} %get-tuple-element.16), channel_id=1, source_target_pairs={{0,32},{32,64},{64,96},{96,128},{128,160},{160,192},{192,224},{1,3... | collective-permute-start | bytes 49160 | tf_op jit(solution)/shard_map/ppermute | solution.py:386
  6.2 10.8 %collective-permute-start.1 = (f32[4,1,1024]{2,1,0:T(1,128)S(1)}, f32[4,1,1024]{2,1,0:T(1,128)S(1)}, u32[]{:S(2)}, u32[]{:S(2)}) collective-permute-start(f32[4,1,1024]{2,1,0:T(1,128)S(1)} %get-tuple-element.17), channel_id=1, source_target_pairs={{32,0},{64,32},{96,64},{128,96},{160,128},{192,160},{224,192},{33,... | collective-permute-start | bytes 49160 | tf_op jit(solution)/shard_map/ppermute | solution.py:389
  10.0 2.0 copy-start.5
  13.1 3.9 %copy-start.4 = (f32[4,128,1024]{2,1,0:T(8,128)S(1)}, f32[4,128,1024]{2,1,0:T(8,128)}, u32[]{:S(2)}) copy-start(f32[4,128,1024]{2,1,0:T(8,128)} %param.11) | copy-start | bytes 6291460
  18.1 14.8 %collective-permute-start.2 = (f32[1,130,1024]{2,1,0:T(8,128)}, f32[1,130,1024]{2,1,0:T(8,128)}, u32[]{:S(2)}, u32[]{:S(2)}) collective-permute-start(f32[1,130,1024]{2,1,0:T(8,128)} %get-tuple-element.10), channel_id=1, source_target_pairs={{0,1},{1,2},{2,3},{3,4},{4,5},{5,6},{6,7},{7,8},{8,9},{9,10},{10,1... | collective-permute-start | bytes 1597448 | tf_op jit(solution)/shard_map/ppermute | solution.py:386
  22.5 15.3 %collective-permute-start.3 = (f32[1,130,1024]{2,1,0:T(8,128)}, f32[1,130,1024]{2,1,0:T(8,128)}, u32[]{:S(2)}, u32[]{:S(2)}) collective-permute-start(f32[1,130,1024]{2,1,0:T(8,128)} %get-tuple-element.11), channel_id=1, source_target_pairs={{1,0},{2,1},{3,2},{4,3},{5,4},{6,5},{7,6},{8,7},{9,8},{10,9},{11,1... | collective-permute-start | bytes 1597448 | tf_op jit(solution)/shard_map/ppermute | solution.py:389
  25.3 12.5 %copy-start.6 = (s32[4,128,1024]{2,1,0:T(8,128)S(1)}, s32[4,128,1024]{2,1,0:T(8,128)}, u32[]{:S(2)}) copy-start(s32[4,128,1024]{2,1,0:T(8,128)} %param.12) | copy-start | bytes 6291460
  25.3 12.5 %copy-start.7 = (f32[128,1024]{1,0:T(8,128)S(1)}, f32[128,1024]{1,0:T(8,128)}, u32[]{:S(2)}) copy-start(f32[128,1024]{1,0:T(8,128)} %get-tuple-element.18) | copy-start | bytes 1572868
  25.3 12.5 %copy-start.8 = (f32[128,1024]{1,0:T(8,128)S(1)}, f32[128,1024]{1,0:T(8,128)}, u32[]{:S(2)}) copy-start(f32[128,1024]{1,0:T(8,128)} %get-tuple-element.19) | copy-start | bytes 1572868
  25.3 12.5 %copy-start.9 = (f32[128,1024]{1,0:T(8,128)S(1)}, f32[128,1024]{1,0:T(8,128)}, u32[]{:S(2)}) copy-start(f32[128,1024]{1,0:T(8,128)} %get-tuple-element.20) | copy-start | bytes 1572868
  25.3 12.5 %copy-start.10 = (f32[4,128,1]{2,1,0:T(8,128)S(1)}, f32[4,128,1]{2,1,0:T(8,128)}, u32[]{:S(2)}) copy-start(f32[4,128,1]{2,1,0:T(8,128)} %get-tuple-element.15) | copy-start | bytes 6148
  25.3 12.5 %copy-start.11 = (f32[128,1024]{1,0:T(8,128)S(1)}, f32[128,1024]{1,0:T(8,128)}, u32[]{:S(2)}) copy-start(f32[128,1024]{1,0:T(8,128)} %param.13) | copy-start | bytes 1572868
  123.9 4.4 %copy-start = (bf16[2,512,512]{2,1,0:T(8,128)(2,1)S(1)}, bf16[2,512,512]{2,1,0:T(8,128)(2,1)}, u32[]{:S(2)}) copy-start(bf16[2,512,512]{2,1,0:T(8,128)(2,1)} %constant.45.clone.to) | copy-start | bytes 3145732
  123.9 4.3 %copy-start.1 = (bf16[2,2,256,256]{3,2,1,0:T(8,128)(2,1)S(1)}, bf16[2,2,256,256]{3,2,1,0:T(8,128)(2,1)}, u32[]{:S(2)}) copy-start(bf16[2,2,256,256]{3,2,1,0:T(8,128)(2,1)} %constant.44.clone.te) | copy-start | bytes 1572868
  123.9 4.3 %copy-start.2 = (f32[1024,128]{1,0:T(8,128)S(1)}, f32[1024,128]{1,0:T(8,128)}, u32[]{:S(2)}) copy-start(f32[1024,128]{1,0:T(8,128)} %constant.47.clone.lam_cols) | copy-start | bytes 1572868
  123.9 4.3 %copy-start.3 = (f32[8,8,128]{2,1,0:T(8,128)S(1)}, f32[8,8,128]{2,1,0:T(8,128)}, u32[]{:S(2)}) copy-start(f32[8,8,128]{2,1,0:T(8,128)} %constant.46.clone.lam_rows) | copy-start | bytes 98308
where the time goes:
time: 206 us
  blocking collectives  79.3 us (38%)
  Pallas kernels  77.6 us (38%)
  other arithmetic  15.2 us (7%)
  starting transfers between devices  12.2 us (6%)
  waiting for transfers between devices  11.7 us (6%)
  local copies, waits for them, and re-layouts  7.68 us (4%)
  between operations  2.22 us (1%)
    psum x1, blocking collectives, per_device(): total_dot = lax.psum(jnp.sum(direction * image), ('row', 'tm'))  79.3 us
    pallas_call x1, Pallas kernels, spectral_solve(): pl.pallas_call(solve_kernel, out_shape=jax.ShapeDtypeStruct((N, FRONT), F...  74.1 us
    ppermute x2, starting transfers between devices, extended_2(): lax.ppermute(lax.slice_in_dim(block, block.shape[dim] - width, None, axis...  8.95 us
    ppermute x2, waiting for transfers between devices, extended_2(): lax.ppermute(lax.slice_in_dim(block, block.shape[dim] - width, None, axis...  6.8 us
    reduce_sum x1, other arithmetic, per_device(): total_dot = lax.psum(jnp.sum(direction * image), ('row', 'tm'))  6.01 us
    ppermute x2, waiting for transfers between devices, extended_2(): lax.ppermute(lax.slice_in_dim(block, 0, width, axis=dim), axis, backward)  4.91 us
    sub x1, other arithmetic, per_device(): residual_new = residual - alpha * image  4.3 us
  transfers between devices with their start and end apart: 4, of which 2 were waited for; matrix products, arithmetic and copies ran while one was open for 4% of the time, Pallas kernels for 0%

commit v1 on v0

--- a/solution.py
+++ b/solution.py
@@ -1,4 +1,3 @@
-import functools
 import math
 
 import jax
@@ -87,13 +86,27 @@
     return pl.multiple_of(start, CK)
 
 
-def solve_kernel(
-    res, te, to, lam_rows, lam_cols, y,
+def step_kernel(
+    direction, residual, observed, obs_weight, blocks, te_in, to_in, lam_rows_in, lam_cols_in, previous,
+    y, res_out,
+    dir_v, res_v, obs_v, wgt_v, blk_v, te, to, lam_rows, lam_cols,
+    image, halo_t, halo_r, ocean, dots, dot_row, dot_z, dot_x,
     r_even, r_odd, v_even, v_odd, send_a, recv_a, spec, fg, own, back, inc, send_w,
+    sem_in, sem_out, sem_hs, sem_hr, sem_ds, sem_dr,
     sem_sa, sem_ra, sem_sf, sem_rf, sem_sb, sem_rb, sem_sw, sem_rw,
 ):
     row = lax.axis_index("row")
     tm = lax.axis_index("tm")
+    loads = [
+        pltpu.make_async_copy(src, dst, sem_in.at[k])
+        for k, (src, dst) in enumerate((
+            (blocks, blk_v), (direction, dir_v), (obs_weight, wgt_v), (observed, obs_v),
+            (residual, res_v), (te_in, te), (to_in, to), (lam_rows_in, lam_rows),
+            (lam_cols_in, lam_cols),
+        ))
+    ]
+    for load in loads:
+        load.start()
 
     barrier = pltpu.get_barrier_semaphore()
 
@@ -109,20 +122,153 @@
             barrier, inc=1, device_id={"tm": lax.rem(tm + o, TM)}, device_id_type=MESH
         )
 
+    def remote(src, dst, send_sem, recv_sem, axis, peer):
+        return pltpu.make_async_remote_copy(
+            src_ref=src, dst_ref=dst, send_sem=send_sem, recv_sem=recv_sem,
+            device_id={axis: peer}, device_id_type=MESH,
+        )
+
+    def wait_for(ref, sem):
+        pltpu.make_async_copy(ref, ref, sem).wait()
+
+    pl.semaphore_wait(barrier, ROWS - 1 + TM - 1)
+    tm_next, tm_prev = lax.rem(tm + 1, TM), lax.rem(tm + TM - 1, TM)
+    row_next, row_prev = lax.rem(row + 1, ROWS), lax.rem(row + ROWS - 1, ROWS)
+    halos = [
+        remote(direction.at[HOURS - 1], halo_t.at[0], sem_hs.at[0], sem_hr.at[0], "tm", tm_next),
+        remote(direction.at[0], halo_t.at[1], sem_hs.at[1], sem_hr.at[1], "tm", tm_prev),
+        remote(
+            direction.at[:, pl.ds(BAND - 8, 8), :], halo_r.at[0], sem_hs.at[2], sem_hr.at[2],
+            "row", row_next,
+        ),
+        remote(
+            direction.at[:, pl.ds(0, 8), :], halo_r.at[1], sem_hs.at[3], sem_hr.at[3],
+            "row", row_prev,
+        ),
+    ]
+    for halo in halos:
+        halo.start()
+
+    loads[0].wait()
+    spread = (
+        lax.broadcasted_iota(jnp.int32, (N // BLOCK, N), 1) // BLOCK
+        == lax.broadcasted_iota(jnp.int32, (N // BLOCK, N), 0)
+    ).astype(F32).astype(BF16)
+    ocean[0:8, :] = jnp.zeros((8, N), F32)
+    ocean[136:144, :] = jnp.zeros((8, N), F32)
+    ocean[8:136, :] = lax.dot_general(
+        blk_v[...].astype(F32).astype(BF16), spread, NN, preferred_element_type=F32
+    )
+    for k in (1, 2, 3):
+        loads[k].wait()
+
+    sub = lax.broadcasted_iota(jnp.int32, (8, N), 0)
+
+    def wide(i):
+        return jnp.broadcast_to(ocean[pl.ds(row * (BAND // BLOCK) + i + 8, 1), :], (8, N))
+
+    def strip(i, above, below, acc):
+        here = pl.ds(pl.multiple_of(i * 8, 8), 8)
+        sea, sea_up, sea_down = wide(i), wide(i - 1), wide(i + 1)
+        north_link = sea * jnp.where(sub == 0, sea_up, sea)
+        south_link = sea * jnp.where(sub == 7, sea_down, sea)
+        east_link = sea * pltpu.roll(sea, N - 1, 1)
+        sea_weight = sea * wgt_v[here, :]
+        v = [dir_v[h, here, :] for h in range(HOURS)]
+        for h in range(HOURS):
+            north = jnp.where(sub == 0, pltpu.roll(above(h), 1, 0), pltpu.roll(v[h], 1, 0))
+            south = jnp.where(sub == 7, pltpu.roll(below(h), 7, 0), pltpu.roll(v[h], 7, 0))
+            flux = east_link * (v[h] - pltpu.roll(v[h], N - 1, 1))
+            value = (obs_v[h, here, :].astype(F32) * sea_weight + NUGGET) * v[h]
+            value += north_link * (v[h] - north) + south_link * (v[h] - south)
+            value += flux - pltpu.roll(flux, 1, 1)
+            near = [v[h] - v[k] for k in (h - 1, h + 1) if 0 <= k < HOURS]
+            value += COUPLING * (near[0] + near[1] if len(near) == 2 else near[0])
+            image[h, here, :] = value
+            acc += value * v[h]
+        return acc
+
+    def inner(i, acc):
+        above = pl.ds(pl.multiple_of(i * 8 - 8, 8), 8)
+        below = pl.ds(pl.multiple_of(i * 8 + 8, 8), 8)
+        return strip(i, lambda h: dir_v[h, above, :], lambda h: dir_v[h, below, :], acc)
+
+    strips = BAND // 8
+    acc = lax.fori_loop(1, strips - 1, inner, jnp.zeros((8, N), F32))
+    wait_for(halo_r.at[0], sem_hr.at[2])
+    acc = strip(0, lambda h: halo_r[0, h], lambda h: dir_v[h, 8:16, :], acc)
+    wait_for(halo_r.at[1], sem_hr.at[3])
+    acc = strip(
+        strips - 1, lambda h: dir_v[h, BAND - 16:BAND - 8, :], lambda h: halo_r[1, h], acc
+    )
+
+    wait_for(halo_t.at[0], sem_hr.at[0])
+    wait_for(halo_t.at[1], sem_hr.at[1])
+    hour_links = (
+        jnp.full((8, N), jnp.where(tm > 0, COUPLING, 0.0), F32),
+        jnp.full((8, N), jnp.where(tm < TM - 1, COUPLING, 0.0), F32),
+    )
+
+    def outer(i, acc):
+        here = pl.ds(pl.multiple_of(i * 8, 8), 8)
+        for side, h in ((0, 0), (1, HOURS - 1)):
+            v = dir_v[h, here, :]
+            extra = hour_links[side] * (v - halo_t[side, here, :])
+            image[h, here, :] += extra
+            acc += extra * v
+        return acc
+
+    acc = lax.fori_loop(0, strips, outer, acc)
+
+    tile = acc[:, 0:128]
+    for l in range(1, 8):
+        tile += acc[:, l * 128:(l + 1) * 128]
+
+    def share(tile, k, buf, count, me, axis, peer_of):
+        dots[k] = tile
+        buf[me] = tile
+
+        @pl.loop(1, count)
+        def _(o):
+            remote(
+                dots.at[k], buf.at[me], sem_ds.at[k], sem_dr.at[k], axis, peer_of(o)
+            ).start()
+
+        wait_for(buf.at[pl.ds(0, count - 1)], sem_dr.at[k])
+        total = buf[0]
+        for j in range(1, count):
+            total += buf[j]
+        return total
+
+    x, z = tm // 8, tm % 8
+    tile = share(tile, 0, dot_row, ROWS, row, "row", lambda o: lax.rem(row + o, ROWS))
+    tile = share(tile, 1, dot_z, 8, z, "tm", lambda o: x * 8 + lax.rem(z + o, 8))
+    tile = share(tile, 2, dot_x, 4, x, "tm", lambda o: lax.rem(x + o, 4) * 8 + z)
+    total = jnp.sum(jnp.sum(tile, axis=1, keepdims=True), axis=0, keepdims=True)
+    alpha = previous[0] / (total / float(NT * N * N))
+
+    for k in range(4, 9):
+        loads[k].wait()
     for h in range(HOURS):
-        rows = slice(h * BAND, (h + 1) * BAND)
-        low = res[rows, 0:512]
-        high = res[rows, 512:1024]
-        hi, lo = split(low - high)
-        r_odd[0, rows, :] = hi
-        r_odd[1, rows, :] = lo
-        even = low + high
-        for s, value in ((0, even[:, :256] + even[:, 256:]), (1, even[:, :256] - even[:, 256:])):
-            hi, lo = split(value)
-            r_even[s, 0, rows, :] = hi
-            r_even[s, 1, rows, :] = lo
-
-    pl.semaphore_wait(barrier, ROWS - 1 + TM - 1)
+        @pl.loop(0, BAND // 16)
+        def _(i):
+            here = pl.ds(pl.multiple_of(i * 16, 16), 16)
+            rows = pl.ds(pl.multiple_of(h * BAND + i * 16, 16), 16)
+            value = res_v[h, here, :] - alpha * image[h, here, :]
+            image[h, here, :] = value
+            low = value[:, 0:512]
+            high = value[:, 512:1024]
+            hi, lo = split(low - high)
+            r_odd[0, rows, :] = hi
+            r_odd[1, rows, :] = lo
+            even = low + high
+            for s, part in ((0, even[:, :256] + even[:, 256:]), (1, even[:, :256] - even[:, 256:])):
+                hi, lo = split(part)
+                r_even[s, 0, rows, :] = hi
+                r_even[s, 1, rows, :] = lo
+
+    store = pltpu.make_async_copy(image, res_out, sem_out.at[0])
+    store.start()
 
     def stage_a(c):
         part = pl.ds(pl.multiple_of(c * (4 * CK), 4 * CK), 4 * CK)
@@ -149,9 +295,6 @@
                 device_id={"row": peer},
                 device_id_type=MESH,
             ).start()
-
-    def wait_for(ref, sem):
-        pltpu.make_async_copy(ref, ref, sem).wait()
 
     def stage_b(c):
         wait_for(recv_a.at[c, pl.ds(0, ROWS - 1)], sem_ra.at[c])
@@ -319,15 +462,39 @@
         wait_for(send_w.at[c, pl.ds(0, ROWS - 1)], sem_sw.at[c])
         wait_for(send_w.at[c, pl.ds(0, ROWS - 1)], sem_rw.at[c])
 
-
-def spectral_solve(res, te, to, lam_rows, lam_cols):
-    vmem = pl.BlockSpec(memory_space=pltpu.VMEM)
+    for k, halo in enumerate(halos):
+        halo.wait_send()
+    for k, count in enumerate((ROWS, 8, 4)):
+        wait_for(dot_row.at[pl.ds(0, count - 1)], sem_ds.at[k])
+    store.wait()
+
+
+def step(direction, residual, observed, obs_weight, blocks, te, to, lam_rows, lam_cols, previous):
+    anywhere = pl.BlockSpec(memory_space=pl.ANY)
+    field = (HOURS, BAND, N)
     return pl.pallas_call(
-        solve_kernel,
-        out_shape=jax.ShapeDtypeStruct((N, FRONT), F32),
-        in_specs=[vmem] * 5,
-        out_specs=vmem,
+        step_kernel,
+        out_shape=(jax.ShapeDtypeStruct((N, FRONT), F32), jax.ShapeDtypeStruct(field, F32)),
+        in_specs=[anywhere] * 9 + [pl.BlockSpec(memory_space=pltpu.SMEM)],
+        out_specs=(pl.BlockSpec(memory_space=pltpu.VMEM), anywhere),
         scratch_shapes=[
+            pltpu.VMEM(field, F32),
+            pltpu.VMEM(field, F32),
+            pltpu.VMEM(field, jnp.int32),
+            pltpu.VMEM((BAND, N), F32),
+            pltpu.VMEM((N // BLOCK, N // BLOCK), jnp.int32),
+            pltpu.VMEM((2, 2, 256, 256), BF16),
+            pltpu.VMEM((2, 512, 512), BF16),
+            pltpu.VMEM((8, 8, 128), F32),
+            pltpu.VMEM((N, 128), F32),
+            pltpu.VMEM(field, F32),
+            pltpu.VMEM((2, BAND, N), F32),
+            pltpu.VMEM((2, HOURS, 8, N), F32),
+            pltpu.VMEM((N // BLOCK + 16, N), F32),
+            pltpu.VMEM((3, 8, 128), F32),
+            pltpu.VMEM((8, 8, 128), F32),
+            pltpu.VMEM((8, 8, 128), F32),
+            pltpu.VMEM((4, 8, 128), F32),
             pltpu.VMEM((2, 2, FRONT, 256), BF16),
             pltpu.VMEM((2, FRONT, 512), BF16),
             pltpu.VMEM((2, 2, M, 256), BF16),
@@ -340,13 +507,19 @@
             pltpu.VMEM((CHUNKS, TM, 16, 128), F32),
             pltpu.VMEM((CHUNKS, TM, 16, 128), F32),
             pltpu.VMEM((CHUNKS, ROWS, CK, FRONT), F32),
+            pltpu.SemaphoreType.DMA((9,)),
+            pltpu.SemaphoreType.DMA((1,)),
+            pltpu.SemaphoreType.DMA((4,)),
+            pltpu.SemaphoreType.DMA((4,)),
+            pltpu.SemaphoreType.DMA((3,)),
+            pltpu.SemaphoreType.DMA((3,)),
         ]
         + [pltpu.SemaphoreType.DMA((CHUNKS,))] * 8,
         compiler_params=pltpu.CompilerParams(
-            collective_id=1, has_side_effects=True, vmem_limit_bytes=48 * 1024 * 1024
+            collective_id=1, has_side_effects=True, vmem_limit_bytes=60 * 1024 * 1024
         ),
-        name="spectral_solve",
-    )(res, te, to, lam_rows, lam_cols)
+        name="step",
+    )(direction, residual, observed, obs_weight, blocks, te, to, lam_rows, lam_cols, previous)
 
 
 def finish_kernel(y, te, to, out):
@@ -378,62 +551,13 @@
     )(y, te, to)
 
 
-def extended_2(block, sides, width):
-    for axis, dim in sides:
-        count = lax.axis_size(axis)
-        forward = [(i, i + 1) for i in range(count - 1)]
-        backward = [(target, source) for source, target in forward]
-        low = lax.ppermute(
-            lax.slice_in_dim(block, block.shape[dim] - width, None, axis=dim), axis, forward
-        )
-        high = lax.ppermute(lax.slice_in_dim(block, 0, width, axis=dim), axis, backward)
-        block = jnp.concatenate([low, block, high], axis=dim)
-    return block
-
-
 def per_device(residual, direction, observed, obs_weight, ocean_blocks, previous_dot):
-    hours, rows, cols = direction.shape
-    row_index = lax.axis_index("row")
-    hour_index = lax.axis_index("tm")
-    row_count = lax.axis_size("row")
-    hour_count = lax.axis_size("tm")
-    total_hours = hours * hour_count
-    total_rows = rows * row_count
-    widened = jnp.repeat(ocean_blocks, BLOCK, axis=1).astype(jnp.float32)
-    padded_blocks = jnp.pad(widened, ((1, 1), (0, 0)))
-    cell_rows = jnp.repeat(padded_blocks, BLOCK, axis=0)
-    ocean_rim = lax.dynamic_slice_in_dim(cell_rows, row_index * rows + BLOCK - 1, rows + 2, 0)
-    ocean = ocean_rim[1:-1]
-    north_link = ocean * ocean_rim[:-2]
-    south_link = ocean * ocean_rim[2:]
-    east_link = ocean * jnp.roll(ocean, -1, axis=1)
-    west_link = ocean * jnp.roll(ocean, 1, axis=1)
-    extended = extended_2(direction, (("row", 1), ("tm", 0)), 1)
-    time_prev = extended[:-2, 1:-1]
-    time_next = extended[2:, 1:-1]
-    north = extended[1:-1, :-2]
-    south = extended[1:-1, 2:]
-    east = jnp.roll(direction, -1, axis=2)
-    west = jnp.roll(direction, 1, axis=2)
-    hour_ids = hour_index * hours + jnp.arange(hours, dtype=jnp.int32)
-    has_prev = (hour_ids > 0).astype(jnp.float32)[:, None, None]
-    has_next = (hour_ids < total_hours - 1).astype(jnp.float32)[:, None, None]
-    temporal = has_prev * (direction - time_prev) + has_next * (direction - time_next)
-    weight = observed.astype(jnp.float32) * ocean * obs_weight + NUGGET
-    spatial = (
-        north_link * (direction - north)
-        + south_link * (direction - south)
-        + east_link * (direction - east)
-        + west_link * (direction - west)
-    )
-    image = weight * direction + spatial + COUPLING * temporal
-    total_dot = lax.psum(jnp.sum(direction * image), ("row", "tm"))
-    alpha = previous_dot[0] / (total_dot / float(total_hours * total_rows * cols))
-    residual_new = residual - alpha * image
     te, to, lam_rows, lam_cols = (jnp.asarray(t) for t in tables())
-    y = spectral_solve(residual_new.reshape(FRONT, N), te, to, lam_rows, lam_cols)
-    precond = finish(y, te, to)
-    return (residual_new, precond)
+    y, residual_new = step(
+        direction, residual, observed, obs_weight, ocean_blocks, te, to, lam_rows, lam_cols,
+        previous_dot,
+    )
+    return (residual_new, finish(y, te, to))
 
 
 def solution(mesh):

time: 206 us -> 116 us (0.56)
  blocking collectives: 79.3 us -> 0 us
  Pallas kernels: 77.6 us -> 112 us
  other arithmetic: 15.2 us -> 0 us
  starting transfers between devices: 12.2 us -> 0 us
  waiting for transfers between devices: 11.7 us -> 0 us
  local copies, waits for them, and re-layouts: 7.68 us -> 2.92 us
    psum x1 -> x0, blocking collectives: 79.3 us -> none  [per_device(): total_dot = lax.psum(jnp.sum(direction * image), ('row', 'tm'))]
    pallas_call x1, Pallas kernels: 74.1 us -> 108 us  [step(): pl.pallas_call(step_kernel, out_shape=(jax.ShapeDtypeStruct((N, FRONT), F...]
    ppermute x4 -> x0, starting transfers between devices: 12.2 us -> none  [the longest x2 8.95 us: extended_2(): lax.ppermute(lax.slice_in_dim(block, block.shape[dim] - width, None, axis...]
    ppermute x4 -> x0, waiting for transfers between devices: 11.7 us -> none  [the longest x2 6.8 us: extended_2(): lax.ppermute(lax.slice_in_dim(block, block.shape[dim] - width, None, axis...]
    reduce_sum x1 -> x0, other arithmetic: 6.01 us -> none  [per_device(): total_dot = lax.psum(jnp.sum(direction * image), ('row', 'tm'))]
    slice x5 -> x0, local copies, waits for them, and re-layouts: 4.81 us -> none  [the longest x2 2.23 us: per_device(): east_link = ocean * jnp.roll(ocean, -1, axis=1)]
    sub x1 -> x0, other arithmetic: 4.3 us -> none  [per_device(): residual_new = residual - alpha * image]
    mul x2 -> x0, other arithmetic: 2.89 us -> none  [the longest x1 2.79 us: per_device(): south_link = ocean * ocean_rim[2:]]
  transfers between devices with their start and end apart: 4 -> 0, of which waited for: 2 -> 0; matrix products, arithmetic and copies ran while one was open for 4% -> 0% of each run, Pallas kernels for 0% -> 0%
where the time goes in v1:
time: 116 us
  Pallas kernels  112 us (97%)
  local copies, waits for them, and re-layouts  2.92 us (3%)
  between operations  1.33 us (1%)
    pallas_call x1, Pallas kernels, step(): pl.pallas_call(step_kernel, out_shape=(jax.ShapeDtypeStruct((N, FRONT), F...  108 us
    pallas_call x1, Pallas kernels, finish(): pl.pallas_call(finish_kernel, grid=(HOURS,), out_shape=jax.ShapeDtypeStru...  3.41 us
    unnamed x9, local copies, waits for them, and re-layouts  2.92 us

profile of v1, /device:TPU:1, one launch (start us, length us, event | category | flops | bytes accessed | tf_op | source)
XLA Modules:
  0.0 115.8 jit_solution(2881635712088013195)
XLA Ops:
  1.3 0.0 copy-start
  1.3 0.0 copy-start.2
  1.3 108.2 %step.1 = (f32[1024,512]{1,0:T(8,128)}, f32[4,128,1024]{2,1,0:T(8,128)}) custom-call(f32[4,128,1024]{2,1,0:T(8,128)} %direction.1, f32[4,128,1024]{2,1,0:T(8,128)} %residual.1, s32[4,128,1024]{2,1,0:T(8,128)} %observed.1, f32[128,1024]{1,0:T(8,128)} %obs_weight.1, s32[128,128]{1,0:T(8,128)} %blocks.1, bf16[2,2,256,256]{3,2,1,0:T(8,128)(2,1)} %constant.8.clone.te_in.te, ...), custom_call_target="tpu_custom_call" | custom-call | tf_op jit(solution)/shard_map/step/pallas_call | solution.py:475
  109.5 0.0 copy-done
  109.5 0.0 copy-done.2
  109.5 0.0 copy-start.1
  109.5 1.6 %copy-done.1 = f32[1024,512]{1,0:T(8,128)S(1)} copy-done((f32[1024,512]{1,0:T(8,128)S(1)}, f32[1024,512]{1,0:T(8,128)}, u32[]{:S(2)}) %copy-start.1) | copy-done | bytes 2097176
  111.1 0.0 copy-start.3
  111.1 3.4 %finish.1 = f32[4,128,1024]{2,1,0:T(8,128)} custom-call(f32[1024,512]{1,0:T(8,128)S(1)} %copy-done.1, bf16[2,2,256,256]{3,2,1,0:T(8,128)(2,1)S(1)} %copy-done.2, bf16[2,512,512]{2,1,0:T(8,128)(2,1)S(1)} %copy-done), custom_call_target="tpu_custom_call" | custom-call | tf_op jit(solution)/shard_map/finish/pallas_call | solution.py:539
  114.5 0.0 copy-done.3
  114.5 1.3 %copy.14 = f32[4,128,1024]{2,1,0:T(8,128)} copy(f32[4,128,1024]{2,1,0:T(8,128)S(1)} %copy-done.3) | data formatting | bytes 4194304
Async XLA Ops:
  1.3 108.2 %copy-start = (bf16[2,512,512]{2,1,0:T(8,128)(2,1)S(1)}, bf16[2,512,512]{2,1,0:T(8,128)(2,1)}, u32[]{:S(2)}) copy-start(bf16[2,512,512]{2,1,0:T(8,128)(2,1)} %constant.9.clone.to_in.to) | copy-start | bytes 3145732
  1.3 108.2 %copy-start.2 = (bf16[2,2,256,256]{3,2,1,0:T(8,128)(2,1)S(1)}, bf16[2,2,256,256]{3,2,1,0:T(8,128)(2,1)}, u32[]{:S(2)}) copy-start(bf16[2,2,256,256]{3,2,1,0:T(8,128)(2,1)} %constant.8.clone.te_in.te) | copy-start | bytes 1572868
  109.5 1.6 %copy-start.1 = (f32[1024,512]{1,0:T(8,128)S(1)}, f32[1024,512]{1,0:T(8,128)}, u32[]{:S(2)}) copy-start(f32[1024,512]{1,0:T(8,128)} %get-tuple-element.5.y) | copy-start | bytes 6291460
  111.1 3.4 %copy-start.3 = (f32[4,128,1024]{2,1,0:T(8,128)S(1)}, f32[4,128,1024]{2,1,0:T(8,128)}, u32[]{:S(2)}) copy-start(f32[4,128,1024]{2,1,0:T(8,128)} %get-tuple-element.8) | copy-start | bytes 6291460

commit v2 on v1

--- a/solution.py
+++ b/solution.py
@@ -90,9 +90,9 @@
     direction, residual, observed, obs_weight, blocks, te_in, to_in, lam_rows_in, lam_cols_in, previous,
     y, res_out,
     dir_v, res_v, obs_v, wgt_v, blk_v, te, to, lam_rows, lam_cols,
-    image, halo_t, halo_r, ocean, dots, dot_row, dot_z, dot_x,
-    r_even, r_odd, v_even, v_odd, send_a, recv_a, spec, fg, own, back, inc, send_w,
-    sem_in, sem_out, sem_hs, sem_hr, sem_ds, sem_dr,
+    image, halo_t, halo_r, ocean, dots, dot_row, dot_tm,
+    r_even, r_odd, v_even, v_odd, send_r, recv_r, send_a, recv_a, spec, fg, own, back, inc, send_w,
+    sem_in, sem_out, sem_hs, sem_hr, sem_ds, sem_dr, sem_sr, sem_rr,
     sem_sa, sem_ra, sem_sf, sem_rf, sem_sb, sem_rb, sem_sw, sem_rw,
 ):
     row = lax.axis_index("row")
@@ -134,17 +134,27 @@
     pl.semaphore_wait(barrier, ROWS - 1 + TM - 1)
     tm_next, tm_prev = lax.rem(tm + 1, TM), lax.rem(tm + TM - 1, TM)
     row_next, row_prev = lax.rem(row + 1, ROWS), lax.rem(row + ROWS - 1, ROWS)
+    half = BAND // 2
+
+    def slab(k, hour, start, side, peer):
+        rows = pl.ds(start, half)
+        return remote(
+            direction.at[hour, rows], halo_t.at[side, rows], sem_hs.at[k], sem_hr.at[k], "tm", peer
+        )
+
     halos = [
-        remote(direction.at[HOURS - 1], halo_t.at[0], sem_hs.at[0], sem_hr.at[0], "tm", tm_next),
-        remote(direction.at[0], halo_t.at[1], sem_hs.at[1], sem_hr.at[1], "tm", tm_prev),
         remote(
-            direction.at[:, pl.ds(BAND - 8, 8), :], halo_r.at[0], sem_hs.at[2], sem_hr.at[2],
+            direction.at[:, pl.ds(BAND - 8, 8), :], halo_r.at[0], sem_hs.at[4], sem_hr.at[4],
             "row", row_next,
         ),
         remote(
-            direction.at[:, pl.ds(0, 8), :], halo_r.at[1], sem_hs.at[3], sem_hr.at[3],
+            direction.at[:, pl.ds(0, 8), :], halo_r.at[1], sem_hs.at[5], sem_hr.at[5],
             "row", row_prev,
         ),
+        slab(0, HOURS - 1, half, 0, tm_next),
+        slab(1, 0, 0, 1, tm_prev),
+        slab(2, HOURS - 1, 0, 0, tm_next),
+        slab(3, 0, half, 1, tm_prev),
     ]
     for halo in halos:
         halo.start()
@@ -159,6 +169,53 @@
     ocean[8:136, :] = lax.dot_general(
         blk_v[...].astype(F32).astype(BF16), spread, NN, preferred_element_type=F32
     )
+    def prepare(source):
+        for h in range(HOURS):
+            @pl.loop(0, BAND // 16)
+            def _(i):
+                here = pl.ds(pl.multiple_of(i * 16, 16), 16)
+                rows = pl.ds(pl.multiple_of(h * BAND + i * 16, 16), 16)
+                value = source[h, here, :]
+                low = value[:, 0:512]
+                high = value[:, 512:1024]
+                hi, lo = split(low - high)
+                r_odd[0, rows, :] = hi
+                r_odd[1, rows, :] = lo
+                even = low + high
+                for s, part in (
+                    (0, even[:, :256] + even[:, 256:]), (1, even[:, :256] - even[:, 256:])
+                ):
+                    hi, lo = split(part)
+                    r_even[s, 0, rows, :] = hi
+                    r_even[s, 1, rows, :] = lo
+
+    def columns(c, dest):
+        part = pl.ds(pl.multiple_of(c * (4 * CK), 4 * CK), 4 * CK)
+        out = dot3(to[0, part, :], to[1, part, :], r_odd[0], r_odd[1], NT_DIMS)
+        for r in range(4):
+            dest[c, 4 + r] = out[r * CK:(r + 1) * CK]
+        part = pl.ds(pl.multiple_of(c * (2 * CK), 2 * CK), 2 * CK)
+        for s in range(2):
+            out = dot3(
+                te[s, 0, part, :], te[s, 1, part, :], r_even[s, 0], r_even[s, 1], NT_DIMS
+            )
+            for r in range(2):
+                dest[c, 2 * s + r] = out[r * CK:(r + 1) * CK]
+
+    def send_columns(source, dest, send_sem, recv_sem):
+        dest[row] = source[row]
+
+        @pl.loop(1, ROWS)
+        def _(o):
+            peer = lax.rem(row + o, ROWS)
+            remote(source.at[peer], dest.at[row], send_sem, recv_sem, "row", peer).start()
+
+    for k in (4, 5, 6):
+        loads[k].wait()
+    prepare(res_v)
+    columns(0, send_r)
+    send_columns(send_r.at[0], recv_r, sem_sr.at[0], sem_rr.at[0])
+
     for k in (1, 2, 3):
         loads[k].wait()
 
@@ -195,109 +252,100 @@
 
     strips = BAND // 8
     acc = lax.fori_loop(1, strips - 1, inner, jnp.zeros((8, N), F32))
-    wait_for(halo_r.at[0], sem_hr.at[2])
+    wait_for(halo_r.at[0], sem_hr.at[4])
     acc = strip(0, lambda h: halo_r[0, h], lambda h: dir_v[h, 8:16, :], acc)
-    wait_for(halo_r.at[1], sem_hr.at[3])
+    wait_for(halo_r.at[1], sem_hr.at[5])
     acc = strip(
         strips - 1, lambda h: dir_v[h, BAND - 16:BAND - 8, :], lambda h: halo_r[1, h], acc
     )
 
-    wait_for(halo_t.at[0], sem_hr.at[0])
-    wait_for(halo_t.at[1], sem_hr.at[1])
+    @pl.loop(1, CHUNKS)
+    def _(c):
+        columns(c, send_r)
+
     hour_links = (
         jnp.full((8, N), jnp.where(tm > 0, COUPLING, 0.0), F32),
         jnp.full((8, N), jnp.where(tm < TM - 1, COUPLING, 0.0), F32),
     )
-
-    def outer(i, acc):
-        here = pl.ds(pl.multiple_of(i * 8, 8), 8)
-        for side, h in ((0, 0), (1, HOURS - 1)):
-            v = dir_v[h, here, :]
-            extra = hour_links[side] * (v - halo_t[side, here, :])
-            image[h, here, :] += extra
-            acc += extra * v
-        return acc
-
-    acc = lax.fori_loop(0, strips, outer, acc)
+    for side, start in ((0, half), (1, 0)):
+        wait_for(halo_t.at[side, pl.ds(start, half)], sem_hr.at[side])
+
+        def across(i, acc, side=side, start=start):
+            here = pl.ds(pl.multiple_of(start + i * 8, 8), 8)
+            jump = dir_v[side * (HOURS - 1), here, :] - halo_t[side, here, :]
+            return acc + hour_links[side] * (jump * jump)
+
+        acc = lax.fori_loop(0, half // 8, across, acc)
 
     tile = acc[:, 0:128]
     for l in range(1, 8):
         tile += acc[:, l * 128:(l + 1) * 128]
 
-    def share(tile, k, buf, count, me, axis, peer_of):
+    def share(tile, k, buf, count, me, axis):
         dots[k] = tile
         buf[me] = tile
 
         @pl.loop(1, count)
         def _(o):
-            remote(
-                dots.at[k], buf.at[me], sem_ds.at[k], sem_dr.at[k], axis, peer_of(o)
-            ).start()
-
+            peer = lax.rem(me + o, count)
+            remote(dots.at[k], buf.at[me], sem_ds.at[k], sem_dr.at[k], axis, peer).start()
+
+    def gather(k, buf, count):
         wait_for(buf.at[pl.ds(0, count - 1)], sem_dr.at[k])
         total = buf[0]
         for j in range(1, count):
             total += buf[j]
         return total
 
-    x, z = tm // 8, tm % 8
-    tile = share(tile, 0, dot_row, ROWS, row, "row", lambda o: lax.rem(row + o, ROWS))
-    tile = share(tile, 1, dot_z, 8, z, "tm", lambda o: x * 8 + lax.rem(z + o, 8))
-    tile = share(tile, 2, dot_x, 4, x, "tm", lambda o: lax.rem(x + o, 4) * 8 + z)
+    share(tile, 0, dot_row, ROWS, row, "row")
+    for side, start in ((0, 0), (1, half)):
+        wait_for(halo_t.at[side, pl.ds(start, half)], sem_hr.at[2 + side])
+
+    @pl.loop(0, strips)
+    def _(i):
+        here = pl.ds(pl.multiple_of(i * 8, 8), 8)
+        for side, h in ((0, 0), (1, HOURS - 1)):
+            image[h, here, :] += hour_links[side] * (dir_v[h, here, :] - halo_t[side, here, :])
+
+    share(gather(0, dot_row, ROWS), 1, dot_tm, TM, tm, "tm")
+    prepare(image)
+    columns(0, send_a)
+    send_columns(send_a.at[0], recv_a.at[0], sem_sa.at[0], sem_ra.at[0])
+
+    @pl.loop(1, CHUNKS)
+    def _(c):
+        columns(c, send_a)
+
+    tile = gather(1, dot_tm, TM)
     total = jnp.sum(jnp.sum(tile, axis=1, keepdims=True), axis=0, keepdims=True)
     alpha = previous[0] / (total / float(NT * N * N))
 
-    for k in range(4, 9):
-        loads[k].wait()
-    for h in range(HOURS):
-        @pl.loop(0, BAND // 16)
-        def _(i):
-            here = pl.ds(pl.multiple_of(i * 16, 16), 16)
-            rows = pl.ds(pl.multiple_of(h * BAND + i * 16, 16), 16)
-            value = res_v[h, here, :] - alpha * image[h, here, :]
-            image[h, here, :] = value
-            low = value[:, 0:512]
-            high = value[:, 512:1024]
-            hi, lo = split(low - high)
-            r_odd[0, rows, :] = hi
-            r_odd[1, rows, :] = lo
-            even = low + high
-            for s, part in ((0, even[:, :256] + even[:, 256:]), (1, even[:, :256] - even[:, 256:])):
-                hi, lo = split(part)
-                r_even[s, 0, rows, :] = hi
-                r_even[s, 1, rows, :] = lo
+    @pl.loop(1, CHUNKS)
+    def _(c):
+        for r in range(ROWS):
+            send_a[c, r] = send_r[c, r] - alpha * send_a[c, r]
+        send_columns(send_a.at[c], recv_a.at[c], sem_sa.at[c], sem_ra.at[c])
+
+    @pl.loop(0, strips)
+    def _(i):
+        here = pl.ds(pl.multiple_of(i * 8, 8), 8)
+        for h in range(HOURS):
+            image[h, here, :] = res_v[h, here, :] - alpha * image[h, here, :]
 
     store = pltpu.make_async_copy(image, res_out, sem_out.at[0])
     store.start()
-
-    def stage_a(c):
-        part = pl.ds(pl.multiple_of(c * (4 * CK), 4 * CK), 4 * CK)
-        out = dot3(to[0, part, :], to[1, part, :], r_odd[0], r_odd[1], NT_DIMS)
-        for r in range(4):
-            send_a[c, 4 + r] = out[r * CK:(r + 1) * CK]
-        part = pl.ds(pl.multiple_of(c * (2 * CK), 2 * CK), 2 * CK)
-        for s in range(2):
-            out = dot3(
-                te[s, 0, part, :], te[s, 1, part, :], r_even[s, 0], r_even[s, 1], NT_DIMS
-            )
-            for r in range(2):
-                send_a[c, 2 * s + r] = out[r * CK:(r + 1) * CK]
-        recv_a[c, row] = send_a[c, row]
-
-        @pl.loop(1, ROWS)
-        def _(o):
-            peer = lax.rem(row + o, ROWS)
-            pltpu.make_async_remote_copy(
-                src_ref=send_a.at[c, peer],
-                dst_ref=recv_a.at[c, row],
-                send_sem=sem_sa.at[c],
-                recv_sem=sem_ra.at[c],
-                device_id={"row": peer},
-                device_id_type=MESH,
-            ).start()
+    for k in (7, 8):
+        loads[k].wait()
+    wait_for(recv_r.at[pl.ds(0, ROWS - 1)], sem_rr.at[0])
+    wait_for(recv_a.at[0, pl.ds(0, ROWS - 1)], sem_ra.at[0])
+    for r in range(ROWS):
+        recv_a[0, r] = recv_r[r] - alpha * recv_a[0, r]
 
     def stage_b(c):
-        wait_for(recv_a.at[c, pl.ds(0, ROWS - 1)], sem_ra.at[c])
+        @pl.when(c > 0)
+        def _():
+            wait_for(recv_a.at[c, pl.ds(0, ROWS - 1)], sem_ra.at[c])
+
         for h in range(HOURS):
             rows = slice(h * CK, (h + 1) * CK)
             lanes = slice(h * BAND, (h + 1) * BAND)
@@ -434,10 +482,6 @@
                 device_id_type=MESH,
             ).start()
 
-    @pl.loop(0, CHUNKS)
-    def _(c):
-        stage_a(c)
-
     @pl.loop(0, CHUNKS + 2)
     def _(i):
         @pl.when(i < CHUNKS)
@@ -464,8 +508,9 @@
 
     for k, halo in enumerate(halos):
         halo.wait_send()
-    for k, count in enumerate((ROWS, 8, 4)):
-        wait_for(dot_row.at[pl.ds(0, count - 1)], sem_ds.at[k])
+    wait_for(dot_row.at[pl.ds(0, ROWS - 1)], sem_ds.at[0])
+    wait_for(dot_tm.at[pl.ds(0, TM - 1)], sem_ds.at[1])
+    wait_for(send_r.at[0, pl.ds(0, ROWS - 1)], sem_sr.at[0])
     store.wait()
 
 
@@ -491,14 +536,15 @@
             pltpu.VMEM((2, BAND, N), F32),
             pltpu.VMEM((2, HOURS, 8, N), F32),
             pltpu.VMEM((N // BLOCK + 16, N), F32),
-            pltpu.VMEM((3, 8, 128), F32),
-            pltpu.VMEM((8, 8, 128), F32),
-            pltpu.VMEM((8, 8, 128), F32),
-            pltpu.VMEM((4, 8, 128), F32),
+            pltpu.VMEM((2, 8, 128), F32),
+            pltpu.VMEM((ROWS, 8, 128), F32),
+            pltpu.VMEM((TM, 8, 128), F32),
             pltpu.VMEM((2, 2, FRONT, 256), BF16),
             pltpu.VMEM((2, FRONT, 512), BF16),
             pltpu.VMEM((2, 2, M, 256), BF16),
             pltpu.VMEM((2, M, 512), BF16),
+            pltpu.VMEM((CHUNKS, ROWS, CK, FRONT), F32),
+            pltpu.VMEM((ROWS, CK, FRONT), F32),
             pltpu.VMEM((CHUNKS, ROWS, CK, FRONT), F32),
             pltpu.VMEM((CHUNKS, ROWS, CK, FRONT), F32),
             pltpu.VMEM((CHUNKS, M, N), F32),
@@ -509,10 +555,12 @@
             pltpu.VMEM((CHUNKS, ROWS, CK, FRONT), F32),
             pltpu.SemaphoreType.DMA((9,)),
             pltpu.SemaphoreType.DMA((1,)),
-            pltpu.SemaphoreType.DMA((4,)),
-            pltpu.SemaphoreType.DMA((4,)),
-            pltpu.SemaphoreType.DMA((3,)),
-            pltpu.SemaphoreType.DMA((3,)),
+            pltpu.SemaphoreType.DMA((6,)),
+            pltpu.SemaphoreType.DMA((6,)),
+            pltpu.SemaphoreType.DMA((2,)),
+            pltpu.SemaphoreType.DMA((2,)),
+            pltpu.SemaphoreType.DMA((1,)),
+            pltpu.SemaphoreType.DMA((1,)),
         ]
         + [pltpu.SemaphoreType.DMA((CHUNKS,))] * 8,
         compiler_params=pltpu.CompilerParams(

time: 116 us -> 104 us (0.90)
  Pallas kernels: 112 us -> 99.5 us
    pallas_call x1, Pallas kernels: 108 us -> 96.1 us  [step(): pl.pallas_call(step_kernel, out_shape=(jax.ShapeDtypeStruct((N, FRONT), F...]
where the time goes in v2:
time: 104 us
  Pallas kernels  99.5 us (96%)
  local copies, waits for them, and re-layouts  2.92 us (3%)
  between operations  1.33 us (1%)
    pallas_call x1, Pallas kernels, step(): pl.pallas_call(step_kernel, out_shape=(jax.ShapeDtypeStruct((N, FRONT), F...  96.1 us
    pallas_call x1, Pallas kernels, finish(): pl.pallas_call(finish_kernel, grid=(HOURS,), out_shape=jax.ShapeDtypeStru...  3.42 us
    unnamed x9, local copies, waits for them, and re-layouts  2.92 us

profile of v2, /device:TPU:1, one launch (start us, length us, event | category | flops | bytes accessed | tf_op | source)
XLA Modules:
  0.0 103.8 jit_solution(11919281270852586242)
XLA Ops:
  1.3 0.0 copy-start
  1.3 0.0 copy-start.2
  1.3 96.1 %step.1 = (f32[1024,512]{1,0:T(8,128)}, f32[4,128,1024]{2,1,0:T(8,128)}) custom-call(f32[4,128,1024]{2,1,0:T(8,128)} %direction.1, f32[4,128,1024]{2,1,0:T(8,128)} %residual.1, s32[4,128,1024]{2,1,0:T(8,128)} %observed.1, f32[128,1024]{1,0:T(8,128)} %obs_weight.1, s32[128,128]{1,0:T(8,128)} %blocks.1, bf16[2,2,256,256]{3,2,1,0:T(8,128)(2,1)} %constant.8.clone.te_in.te, ...), custom_call_target="tpu_custom_call" | custom-call | tf_op jit(solution)/shard_map/step/pallas_call | solution.py:520
  97.4 0.0 copy-done
  97.5 0.0 copy-done.2
  97.5 0.0 copy-start.1
  97.5 1.6 %copy-done.1 = f32[1024,512]{1,0:T(8,128)S(1)} copy-done((f32[1024,512]{1,0:T(8,128)S(1)}, f32[1024,512]{1,0:T(8,128)}, u32[]{:S(2)}) %copy-start.1) | copy-done | bytes 2097176
  99.1 0.0 copy-start.3
  99.1 3.4 %finish.1 = f32[4,128,1024]{2,1,0:T(8,128)} custom-call(f32[1024,512]{1,0:T(8,128)S(1)} %copy-done.1, bf16[2,2,256,256]{3,2,1,0:T(8,128)(2,1)S(1)} %copy-done.2, bf16[2,512,512]{2,1,0:T(8,128)(2,1)S(1)} %copy-done), custom_call_target="tpu_custom_call" | custom-call | tf_op jit(solution)/shard_map/finish/pallas_call | solution.py:587
  102.5 0.0 copy-done.3
  102.5 1.3 %copy.14 = f32[4,128,1024]{2,1,0:T(8,128)} copy(f32[4,128,1024]{2,1,0:T(8,128)S(1)} %copy-done.3) | data formatting | bytes 4194304
Async XLA Ops:
  1.3 96.2 %copy-start = (bf16[2,512,512]{2,1,0:T(8,128)(2,1)S(1)}, bf16[2,512,512]{2,1,0:T(8,128)(2,1)}, u32[]{:S(2)}) copy-start(bf16[2,512,512]{2,1,0:T(8,128)(2,1)} %constant.9.clone.to_in.to) | copy-start | bytes 3145732
  1.3 96.2 %copy-start.2 = (bf16[2,2,256,256]{3,2,1,0:T(8,128)(2,1)S(1)}, bf16[2,2,256,256]{3,2,1,0:T(8,128)(2,1)}, u32[]{:S(2)}) copy-start(bf16[2,2,256,256]{3,2,1,0:T(8,128)(2,1)} %constant.8.clone.te_in.te) | copy-start | bytes 1572868
  97.5 1.6 %copy-start.1 = (f32[1024,512]{1,0:T(8,128)S(1)}, f32[1024,512]{1,0:T(8,128)}, u32[]{:S(2)}) copy-start(f32[1024,512]{1,0:T(8,128)} %get-tuple-element.5.y) | copy-start | bytes 6291460
  99.1 3.4 %copy-start.3 = (f32[4,128,1024]{2,1,0:T(8,128)S(1)}, f32[4,128,1024]{2,1,0:T(8,128)}, u32[]{:S(2)}) copy-start(f32[4,128,1024]{2,1,0:T(8,128)} %get-tuple-element.8) | copy-start | bytes 6291460

commit v3 on v2

--- a/solution.py
+++ b/solution.py
@@ -39,6 +39,14 @@
     return np.stack([high, low])
 
 
+def first_place(row, chunk):
+    odd = row // 4
+    half = (row // 2) % 2
+    return odd * (512 + chunk * (4 * CK) + (row - 4) * CK) + (1 - odd) * (
+        half * 256 + chunk * (2 * CK) + (row % 2) * CK
+    )
+
+
 def tables():
     def cas(freq, count):
         phase = (freq[:, None] * np.arange(count)[None, :]) % N
@@ -54,7 +62,11 @@
     lam = (2.0 - 2.0 * np.cos(order * (2.0 * math.pi / N))).astype(np.float32)
     lam_rows = np.broadcast_to(lam.reshape(8, 1, 128), (8, 8, 128)).copy()
     lam_cols = np.broadcast_to(lam[:, None], (N, 128)).copy()
-    return even_table, odd_table, lam_rows, lam_cols
+    places = np.concatenate([
+        int(first_place(r, c)) + np.arange(CK) for c in range(CHUNKS) for r in range(ROWS)
+    ])
+    full_table = split_np(cas(order[places], N)).reshape(2, CHUNKS, ROWS * CK, N)
+    return even_table, odd_table, full_table, lam_rows, lam_cols
 
 
 def dot3(a_hi, a_lo, b_hi, b_lo, dims):
@@ -77,21 +89,15 @@
 
 
 def freq_start(row, chunk):
-    odd = row // 4
-    even = 1 - odd
-    half = (row // 2) % 2
-    start = odd * (512 + chunk * (4 * CK) + (row - 4) * CK) + even * (
-        half * 256 + chunk * (2 * CK) + (row % 2) * CK
-    )
-    return pl.multiple_of(start, CK)
+    return pl.multiple_of(first_place(row, chunk), CK)
 
 
 def step_kernel(
-    direction, residual, observed, obs_weight, blocks, te_in, to_in, lam_rows_in, lam_cols_in, previous,
-    y, res_out,
-    dir_v, res_v, obs_v, wgt_v, blk_v, te, to, lam_rows, lam_cols,
-    image, halo_t, halo_r, ocean, dots, dot_row, dot_tm,
-    r_even, r_odd, v_even, v_odd, send_r, recv_r, send_a, recv_a, spec, fg, own, back, inc, send_w,
+    direction, residual, observed, obs_weight, blocks, te_in, to_in, tf_in, lam_rows_in, lam_cols_in, previous,
+    res_out, pre_out,
+    dir_v, res_v, obs_v, wgt_v, blk_v, te, to, tf, lam_rows, lam_cols,
+    image, drive, halo_t, halo_r, ocean, dots, dot_row, dot_tm,
+    r_even, r_odd, v_even, v_odd, send_r, recv_r, send_a, recv_a, spec, fg, own, back, inc, send_w, recv_w, pre,
     sem_in, sem_out, sem_hs, sem_hr, sem_ds, sem_dr, sem_sr, sem_rr,
     sem_sa, sem_ra, sem_sf, sem_rf, sem_sb, sem_rb, sem_sw, sem_rw,
 ):
@@ -102,7 +108,7 @@
         for k, (src, dst) in enumerate((
             (blocks, blk_v), (direction, dir_v), (obs_weight, wgt_v), (observed, obs_v),
             (residual, res_v), (te_in, te), (to_in, to), (lam_rows_in, lam_rows),
-            (lam_cols_in, lam_cols),
+            (lam_cols_in, lam_cols), (tf_in, tf),
         ))
     ]
     for load in loads:
@@ -156,7 +162,7 @@
         slab(2, HOURS - 1, 0, 0, tm_next),
         slab(3, 0, half, 1, tm_prev),
     ]
-    for halo in halos:
+    for halo in halos[:4]:
         halo.start()
 
     loads[0].wait()
@@ -235,10 +241,13 @@
         for h in range(HOURS):
             north = jnp.where(sub == 0, pltpu.roll(above(h), 1, 0), pltpu.roll(v[h], 1, 0))
             south = jnp.where(sub == 7, pltpu.roll(below(h), 7, 0), pltpu.roll(v[h], 7, 0))
-            flux = east_link * (v[h] - pltpu.roll(v[h], N - 1, 1))
+            north, south, east = v[h] - north, v[h] - south, v[h] - pltpu.roll(v[h], N - 1, 1)
+            flux = east_link * east
             value = (obs_v[h, here, :].astype(F32) * sea_weight + NUGGET) * v[h]
-            value += north_link * (v[h] - north) + south_link * (v[h] - south)
+            value += north_link * north + south_link * south
             value += flux - pltpu.roll(flux, 1, 1)
+            plain = north + south + (east - pltpu.roll(east, 1, 1))
+            drive[h, here, :] = value - (PRECOND_SHIFT * v[h] + plain)
             near = [v[h] - v[k] for k in (h - 1, h + 1) if 0 <= k < HOURS]
             value += COUPLING * (near[0] + near[1] if len(near) == 2 else near[0])
             image[h, here, :] = value
@@ -259,10 +268,6 @@
         strips - 1, lambda h: dir_v[h, BAND - 16:BAND - 8, :], lambda h: halo_r[1, h], acc
     )
 
-    @pl.loop(1, CHUNKS)
-    def _(c):
-        columns(c, send_r)
-
     hour_links = (
         jnp.full((8, N), jnp.where(tm > 0, COUPLING, 0.0), F32),
         jnp.full((8, N), jnp.where(tm < TM - 1, COUPLING, 0.0), F32),
@@ -297,20 +302,19 @@
             total += buf[j]
         return total
 
+    for halo in halos[4:]:
+        halo.start()
     share(tile, 0, dot_row, ROWS, row, "row")
-    for side, start in ((0, 0), (1, half)):
-        wait_for(halo_t.at[side, pl.ds(start, half)], sem_hr.at[2 + side])
-
-    @pl.loop(0, strips)
-    def _(i):
-        here = pl.ds(pl.multiple_of(i * 8, 8), 8)
-        for side, h in ((0, 0), (1, HOURS - 1)):
-            image[h, here, :] += hour_links[side] * (dir_v[h, here, :] - halo_t[side, here, :])
-
-    share(gather(0, dot_row, ROWS), 1, dot_tm, TM, tm, "tm")
-    prepare(image)
+
+    @pl.loop(1, CHUNKS)
+    def _(c):
+        columns(c, send_r)
+
+    prepare(drive)
     columns(0, send_a)
     send_columns(send_a.at[0], recv_a.at[0], sem_sa.at[0], sem_ra.at[0])
+
+    share(gather(0, dot_row, ROWS), 1, dot_tm, TM, tm, "tm")
 
     @pl.loop(1, CHUNKS)
     def _(c):
@@ -320,26 +324,43 @@
     total = jnp.sum(jnp.sum(tile, axis=1, keepdims=True), axis=0, keepdims=True)
     alpha = previous[0] / (total / float(NT * N * N))
 
-    @pl.loop(1, CHUNKS)
-    def _(c):
+    def send_rest(c):
         for r in range(ROWS):
             send_a[c, r] = send_r[c, r] - alpha * send_a[c, r]
         send_columns(send_a.at[c], recv_a.at[c], sem_sa.at[c], sem_ra.at[c])
 
-    @pl.loop(0, strips)
-    def _(i):
-        here = pl.ds(pl.multiple_of(i * 8, 8), 8)
-        for h in range(HOURS):
-            image[h, here, :] = res_v[h, here, :] - alpha * image[h, here, :]
-
-    store = pltpu.make_async_copy(image, res_out, sem_out.at[0])
-    store.start()
+    send_rest(1)
     for k in (7, 8):
         loads[k].wait()
     wait_for(recv_r.at[pl.ds(0, ROWS - 1)], sem_rr.at[0])
     wait_for(recv_a.at[0, pl.ds(0, ROWS - 1)], sem_ra.at[0])
     for r in range(ROWS):
         recv_a[0, r] = recv_r[r] - alpha * recv_a[0, r]
+
+    store = pltpu.make_async_copy(image, res_out, sem_out.at[HOURS])
+
+    def after_first():
+        @pl.loop(2, CHUNKS)
+        def _(c):
+            send_rest(c)
+
+        for side, start in ((0, 0), (1, half)):
+            wait_for(halo_t.at[side, pl.ds(start, half)], sem_hr.at[2 + side])
+
+        @pl.loop(0, strips)
+        def _(i):
+            here = pl.ds(pl.multiple_of(i * 8, 8), 8)
+            for side, h in ((0, 0), (1, HOURS - 1)):
+                image[h, here, :] += hour_links[side] * (dir_v[h, here, :] - halo_t[side, here, :])
+
+        @pl.loop(0, strips)
+        def _(i):
+            here = pl.ds(pl.multiple_of(i * 8, 8), 8)
+            for h in range(HOURS):
+                image[h, here, :] = res_v[h, here, :] - alpha * image[h, here, :]
+
+        store.start()
+        loads[9].wait()
 
     def stage_b(c):
         @pl.when(c > 0)
@@ -467,36 +488,64 @@
                     send_w[c, 4 * half + r, :, h * BAND:(h + 1) * BAND] = value[
                         h * CK:(h + 1) * CK, r * BAND:(r + 1) * BAND
                     ]
-        here = pl.ds(freq_start(row, c), CK)
-        y[here, :] = send_w[c, row]
+        recv_w[c, row] = send_w[c, row]
 
         @pl.loop(1, ROWS)
         def _(o):
             peer = lax.rem(row + o, ROWS)
             pltpu.make_async_remote_copy(
                 src_ref=send_w.at[c, peer],
-                dst_ref=y.at[here, :],
+                dst_ref=recv_w.at[c, row],
                 send_sem=sem_sw.at[c],
                 recv_sem=sem_rw.at[c],
                 device_id={"row": peer},
                 device_id_type=MESH,
             ).start()
 
-    @pl.loop(0, CHUNKS + 2)
+    def stage_g(c):
+        wait_for(recv_w.at[c, pl.ds(0, ROWS - 1)], sem_rw.at[c])
+        for h in range(HOURS):
+            part = jnp.concatenate(
+                [recv_w[c, r, :, h * BAND:(h + 1) * BAND] for r in range(ROWS)], axis=0
+            )
+            hi, lo = split(part.T)
+            out = dot3(hi, lo, tf[0, c], tf[1, c], NN)
+
+            @pl.when(c == 0)
+            def _():
+                pre[h] = out - (COUPLING * alpha) * dir_v[h]
+
+            @pl.when(c > 0)
+            def _():
+                pre[h] += out
+
+            @pl.when(c == CHUNKS - 1)
+            def _():
+                pltpu.make_async_copy(pre.at[h], pre_out.at[h], sem_out.at[h]).start()
+
+    @pl.loop(0, CHUNKS + 3)
     def _(i):
         @pl.when(i < CHUNKS)
         def _():
             stage_b(i)
             stage_c(i)
 
+        @pl.when(i == 0)
+        def _():
+            after_first()
+
         @pl.when((i >= 1) & (i < CHUNKS + 1))
         def _():
             stage_d(i - 1)
 
-        @pl.when(i >= 2)
+        @pl.when((i >= 2) & (i < CHUNKS + 2))
         def _():
             stage_e(i - 2)
             stage_f(i - 2)
+
+        @pl.when(i >= 3)
+        def _():
+            stage_g(i - 3)
 
     @pl.loop(0, CHUNKS)
     def _(c):
@@ -504,7 +553,6 @@
         wait_for(fg.at[c, pl.ds(0, TM - 1)], sem_sf.at[c])
         wait_for(back.at[c, pl.ds(0, TM - 1)], sem_sb.at[c])
         wait_for(send_w.at[c, pl.ds(0, ROWS - 1)], sem_sw.at[c])
-        wait_for(send_w.at[c, pl.ds(0, ROWS - 1)], sem_rw.at[c])
 
     for k, halo in enumerate(halos):
         halo.wait_send()
@@ -512,16 +560,18 @@
     wait_for(dot_tm.at[pl.ds(0, TM - 1)], sem_ds.at[1])
     wait_for(send_r.at[0, pl.ds(0, ROWS - 1)], sem_sr.at[0])
     store.wait()
-
-
-def step(direction, residual, observed, obs_weight, blocks, te, to, lam_rows, lam_cols, previous):
+    for h in range(HOURS):
+        pltpu.make_async_copy(pre.at[h], pre_out.at[h], sem_out.at[h]).wait()
+
+
+def step(direction, residual, observed, obs_weight, blocks, te, to, tf, lam_rows, lam_cols, previous):
     anywhere = pl.BlockSpec(memory_space=pl.ANY)
     field = (HOURS, BAND, N)
     return pl.pallas_call(
         step_kernel,
-        out_shape=(jax.ShapeDtypeStruct((N, FRONT), F32), jax.ShapeDtypeStruct(field, F32)),
-        in_specs=[anywhere] * 9 + [pl.BlockSpec(memory_space=pltpu.SMEM)],
-        out_specs=(pl.BlockSpec(memory_space=pltpu.VMEM), anywhere),
+        out_shape=(jax.ShapeDtypeStruct(field, F32), jax.ShapeDtypeStruct(field, F32)),
+        in_specs=[anywhere] * 10 + [pl.BlockSpec(memory_space=pltpu.SMEM)],
+        out_specs=(anywhere, anywhere),
         scratch_shapes=[
             pltpu.VMEM(field, F32),
             pltpu.VMEM(field, F32),
@@ -530,8 +580,10 @@
             pltpu.VMEM((N // BLOCK, N // BLOCK), jnp.int32),
             pltpu.VMEM((2, 2, 256, 256), BF16),
             pltpu.VMEM((2, 512, 512), BF16),
+            pltpu.VMEM((2, CHUNKS, ROWS * CK, N), BF16),
             pltpu.VMEM((8, 8, 128), F32),
             pltpu.VMEM((N, 128), F32),
+            pltpu.VMEM(field, F32),
             pltpu.VMEM(field, F32),
             pltpu.VMEM((2, BAND, N), F32),
             pltpu.VMEM((2, HOURS, 8, N), F32),
@@ -553,8 +605,10 @@
             pltpu.VMEM((CHUNKS, TM, 16, 128), F32),
             pltpu.VMEM((CHUNKS, TM, 16, 128), F32),
             pltpu.VMEM((CHUNKS, ROWS, CK, FRONT), F32),
-            pltpu.SemaphoreType.DMA((9,)),
-            pltpu.SemaphoreType.DMA((1,)),
+            pltpu.VMEM((CHUNKS, ROWS, CK, FRONT), F32),
+            pltpu.VMEM(field, F32),
+            pltpu.SemaphoreType.DMA((10,)),
+            pltpu.SemaphoreType.DMA((HOURS + 1,)),
             pltpu.SemaphoreType.DMA((6,)),
             pltpu.SemaphoreType.DMA((6,)),
             pltpu.SemaphoreType.DMA((2,)),
@@ -567,45 +621,15 @@
             collective_id=1, has_side_effects=True, vmem_limit_bytes=60 * 1024 * 1024
         ),
         name="step",
-    )(direction, residual, observed, obs_weight, blocks, te, to, lam_rows, lam_cols, previous)
-
-
-def finish_kernel(y, te, to, out):
-    value = y[...].T
-    hi, lo = split(value[:, 512:1024])
-    odd = dot3(hi, lo, to[0], to[1], NN)
-    parts = []
-    for s in range(2):
-        hi, lo = split(value[:, s * 256:(s + 1) * 256])
-        parts.append(dot3(hi, lo, te[s, 0], te[s, 1], NN))
-    even = jnp.concatenate([parts[0] + parts[1], parts[0] - parts[1]], axis=1)
-    out[0, :, 0:512] = even + odd
-    out[0, :, 512:1024] = even - odd
-
-
-def finish(y, te, to):
-    return pl.pallas_call(
-        finish_kernel,
-        grid=(HOURS,),
-        out_shape=jax.ShapeDtypeStruct((HOURS, BAND, N), F32),
-        in_specs=[
-            pl.BlockSpec((N, BAND), lambda h: (0, h)),
-            pl.BlockSpec((2, 2, 256, 256), lambda h: (0, 0, 0, 0)),
-            pl.BlockSpec((2, 512, 512), lambda h: (0, 0, 0)),
-        ],
-        out_specs=pl.BlockSpec((1, BAND, N), lambda h: (h, 0, 0)),
-        compiler_params=pltpu.CompilerParams(vmem_limit_bytes=48 * 1024 * 1024),
-        name="finish",
-    )(y, te, to)
+    )(direction, residual, observed, obs_weight, blocks, te, to, tf, lam_rows, lam_cols, previous)
 
 
 def per_device(residual, direction, observed, obs_weight, ocean_blocks, previous_dot):
-    te, to, lam_rows, lam_cols = (jnp.asarray(t) for t in tables())
-    y, residual_new = step(
-        direction, residual, observed, obs_weight, ocean_blocks, te, to, lam_rows, lam_cols,
+    te, to, tf, lam_rows, lam_cols = (jnp.asarray(t) for t in tables())
+    return step(
+        direction, residual, observed, obs_weight, ocean_blocks, te, to, tf, lam_rows, lam_cols,
         previous_dot,
     )
-    return (residual_new, finish(y, te, to))
 
 
 def solution(mesh):

time: 104 us -> 101 us (0.971)
  Pallas kernels: 99.5 us -> 95.4 us
  local copies, waits for them, and re-layouts: 2.92 us -> 4.63 us
    pallas_call x2 -> x1, Pallas kernels: 99.5 us -> 95.4 us  [step(): pl.pallas_call(step_kernel, out_shape=(jax.ShapeDtypeStruct(field, F32),...]
    unnamed x9 -> x4, local copies, waits for them, and re-layouts: 2.92 us -> 4.63 us
where the time goes in v3:
time: 101 us
  Pallas kernels  95.4 us (94%)
  local copies, waits for them, and re-layouts  4.63 us (5%)
  between operations  1.3 us (1%)
    pallas_call x1, Pallas kernels, step(): pl.pallas_call(step_kernel, out_shape=(jax.ShapeDtypeStruct(field, F32),...  95.4 us
    unnamed x4, local copies, waits for them, and re-layouts  4.63 us

profile of v3, /device:TPU:1, one launch (start us, length us, event | category | flops | bytes accessed | tf_op | source)
XLA Modules:
  0.0 101.3 jit_solution(1710760215575189044)
XLA Ops:
  1.3 95.4 %step.1 = (f32[4,128,1024]{2,1,0:T(8,128)}, f32[4,128,1024]{2,1,0:T(8,128)}) custom-call(f32[4,128,1024]{2,1,0:T(8,128)} %direction.1, f32[4,128,1024]{2,1,0:T(8,128)} %residual.1, s32[4,128,1024]{2,1,0:T(8,128)} %observed.1, f32[128,1024]{1,0:T(8,128)} %obs_weight.1, s32[128,128]{1,0:T(8,128)} %blocks.1, bf16[2,2,256,256]{3,2,1,0:T(8,128)(2,1)} %constant.10.clone.te_in, ...), custom_call_target="tpu_custom_call" | custom-call | tf_op jit(solution)/shard_map/step/pallas_call | solution.py:570
  96.7 0.0 copy-start
  96.7 3.3 %copy.16 = f32[4,128,1024]{2,1,0:T(8,128)} copy(f32[4,128,1024]{2,1,0:T(8,128)} %get-tuple-element.4) | data formatting | bytes 4194304
  100.0 0.0 copy-done
  100.0 1.3 %copy.17 = f32[4,128,1024]{2,1,0:T(8,128)} copy(f32[4,128,1024]{2,1,0:T(8,128)S(1)} %copy-done) | data formatting | bytes 4194304
Async XLA Ops:
  96.7 3.3 %copy-start = (f32[4,128,1024]{2,1,0:T(8,128)S(1)}, f32[4,128,1024]{2,1,0:T(8,128)}, u32[]{:S(2)}) copy-start(f32[4,128,1024]{2,1,0:T(8,128)} %get-tuple-element.5) | copy-start | bytes 6291460

commit v4 on v3

--- a/solution.py
+++ b/solution.py
@@ -97,7 +97,7 @@
     res_out, pre_out,
     dir_v, res_v, obs_v, wgt_v, blk_v, te, to, tf, lam_rows, lam_cols,
     image, drive, halo_t, halo_r, ocean, dots, dot_row, dot_tm,
-    r_even, r_odd, v_even, v_odd, send_r, recv_r, send_a, recv_a, spec, fg, own, back, inc, send_w, recv_w, pre,
+    r_even, r_odd, v_even, v_odd, d_even, d_odd, send_r, recv_r, send_a, recv_a, spec, fg, own, back, inc, send_w, recv_w, pre,
     sem_in, sem_out, sem_hs, sem_hr, sem_ds, sem_dr, sem_sr, sem_rr,
     sem_sa, sem_ra, sem_sf, sem_rf, sem_sb, sem_rb, sem_sw, sem_rw,
 ):
@@ -175,7 +175,7 @@
     ocean[8:136, :] = lax.dot_general(
         blk_v[...].astype(F32).astype(BF16), spread, NN, preferred_element_type=F32
     )
-    def prepare(source):
+    def prepare(source, r_even, r_odd):
         for h in range(HOURS):
             @pl.loop(0, BAND // 16)
             def _(i):
@@ -195,7 +195,7 @@
                     r_even[s, 0, rows, :] = hi
                     r_even[s, 1, rows, :] = lo
 
-    def columns(c, dest):
+    def columns(c, dest, r_even, r_odd):
         part = pl.ds(pl.multiple_of(c * (4 * CK), 4 * CK), 4 * CK)
         out = dot3(to[0, part, :], to[1, part, :], r_odd[0], r_odd[1], NT_DIMS)
         for r in range(4):
@@ -218,8 +218,8 @@
 
     for k in (4, 5, 6):
         loads[k].wait()
-    prepare(res_v)
-    columns(0, send_r)
+    prepare(res_v, r_even, r_odd)
+    columns(0, send_r, r_even, r_odd)
     send_columns(send_r.at[0], recv_r, sem_sr.at[0], sem_rr.at[0])
 
     for k in (1, 2, 3):
@@ -306,19 +306,16 @@
         halo.start()
     share(tile, 0, dot_row, ROWS, row, "row")
 
+    prepare(drive, d_even, d_odd)
+    columns(0, send_a, d_even, d_odd)
+    send_columns(send_a.at[0], recv_a.at[0], sem_sa.at[0], sem_ra.at[0])
+
+    share(gather(0, dot_row, ROWS), 1, dot_tm, TM, tm, "tm")
+
     @pl.loop(1, CHUNKS)
     def _(c):
-        columns(c, send_r)
-
-    prepare(drive)
-    columns(0, send_a)
-    send_columns(send_a.at[0], recv_a.at[0], sem_sa.at[0], sem_ra.at[0])
-
-    share(gather(0, dot_row, ROWS), 1, dot_tm, TM, tm, "tm")
-
-    @pl.loop(1, CHUNKS)
-    def _(c):
-        columns(c, send_a)
+        columns(c, send_r, r_even, r_odd)
+        columns(c, send_a, d_even, d_odd)
 
     tile = gather(1, dot_tm, TM)
     total = jnp.sum(jnp.sum(tile, axis=1, keepdims=True), axis=0, keepdims=True)
@@ -595,6 +592,8 @@
             pltpu.VMEM((2, FRONT, 512), BF16),
             pltpu.VMEM((2, 2, M, 256), BF16),
             pltpu.VMEM((2, M, 512), BF16),
+            pltpu.VMEM((2, 2, FRONT, 256), BF16),
+            pltpu.VMEM((2, FRONT, 512), BF16),
             pltpu.VMEM((CHUNKS, ROWS, CK, FRONT), F32),
             pltpu.VMEM((ROWS, CK, FRONT), F32),
             pltpu.VMEM((CHUNKS, ROWS, CK, FRONT), F32),

time: 101 us -> 102 us (level)
  no operation moved by 1% of the time
where the time goes in v4:
time: 102 us
  Pallas kernels  95.6 us (94%)
  local copies, waits for them, and re-layouts  4.63 us (5%)
  between operations  1.3 us (1%)
    pallas_call x1, Pallas kernels, step(): pl.pallas_call(step_kernel, out_shape=(jax.ShapeDtypeStruct(field, F32),...  95.6 us
    unnamed x4, local copies, waits for them, and re-layouts  4.63 us

profile of v4, /device:TPU:1, one launch (start us, length us, event | category | flops | bytes accessed | tf_op | source)
XLA Modules:
  0.0 101.5 jit_solution(10082093820840583678)
XLA Ops:
  1.3 95.6 %step.1 = (f32[4,128,1024]{2,1,0:T(8,128)}, f32[4,128,1024]{2,1,0:T(8,128)}) custom-call(f32[4,128,1024]{2,1,0:T(8,128)} %direction.1, f32[4,128,1024]{2,1,0:T(8,128)} %residual.1, s32[4,128,1024]{2,1,0:T(8,128)} %observed.1, f32[128,1024]{1,0:T(8,128)} %obs_weight.1, s32[128,128]{1,0:T(8,128)} %blocks.1, bf16[2,2,256,256]{3,2,1,0:T(8,128)(2,1)} %constant.10.clone.te_in, ...), custom_call_target="tpu_custom_call" | custom-call | tf_op jit(solution)/shard_map/step/pallas_call | solution.py:567
  96.9 0.0 copy-start
  96.9 3.3 %copy.16 = f32[4,128,1024]{2,1,0:T(8,128)} copy(f32[4,128,1024]{2,1,0:T(8,128)} %get-tuple-element.4) | data formatting | bytes 4194304
  100.2 0.0 copy-done
  100.2 1.3 %copy.17 = f32[4,128,1024]{2,1,0:T(8,128)} copy(f32[4,128,1024]{2,1,0:T(8,128)S(1)} %copy-done) | data formatting | bytes 4194304
Async XLA Ops:
  96.9 3.3 %copy-start = (f32[4,128,1024]{2,1,0:T(8,128)S(1)}, f32[4,128,1024]{2,1,0:T(8,128)}, u32[]{:S(2)}) copy-start(f32[4,128,1024]{2,1,0:T(8,128)} %get-tuple-element.5) | copy-start | bytes 6291460
